TPU v7x, 32 devices: a whole 2x2x4 slice. The times are simulated.
32 devices in a mesh: seq: 16 (over z, y, core), tensor: 2 (over x).
Axes of the slice: x: 2, y: 2, z: 4, core: 2. Of those that a mesh axis runs over, the one named last changes fastest.
Arguments:
- features: bfloat16 [2048, 3072], P('seq', 'tensor'), may hold values from -6 to 6
- gain: float32 [3072], replicated, may hold values from 0.1 to 1.9
- w_qkv: bfloat16 [3072, 3, 3072], P(None, None, 'tensor'), may hold values from -0.109375 to 0.109375
- rope_factors: float32 [48], replicated, may hold values from 1 to 64
- cache_len: int32 [4], replicated, may hold values from 1 to 12288, as said below
- cache_kv: bfloat16 [192, 128, 2, 3072], P('seq', None, None, 'tensor'), may hold values from -405 to 405, as said below
- block_owner: int32 [192], P('seq'), may hold values from 0 to 4, as said below
- block_base: int32 [192], P('seq'), may hold values from 0 to 12160, as said below
Outputs:
- attended: bfloat16 [2048, 3072], P('seq', 'tensor')
- new_kv: bfloat16 [2048, 2, 3072], P('seq', None, 'tensor')
Inputs may be any that keep to these rules, and one draw needn't show every extreme that they name: `cache_len`: one request has exactly 12288 cached tokens; the others have between 1 and 3072. `block_owner`: request r owns exactly ceil(cache_len[r] / 128) blocks, placed anywhere in the pool; 4 marks a free block, and some blocks are free. `block_base`: the blocks of request r carry the bases 0, 128, 256, ... below cache_len[r], each once; free blocks carry 0. `cache_kv`: stored keys are already rotated.
All inputs are finite; a program needn't handle non-finite values.
Results may differ from a plain program's by a relative error of at most 0.014.
The roundings to bfloat16 on the way count: a program that leaves them out, or rounds other values in their place, can miss the bound.
Values may be sent and summed in bfloat16 or wider, within the bound.
A program may use at most 384 MiB of HBM per device.

v0:
```python
import jax
import jax.numpy as jnp
from jax import lax
from jax.sharding import PartitionSpec as P

EPSILON = 1e-05
NEGATIVE = -1e30
MSCALE = 1.1902380714238083


def rotate(vectors, angles):
    half_dim = vectors.shape[-1] // 2
    front_half = vectors[..., :half_dim]
    back_half = vectors[..., half_dim:]
    cosine = jnp.cos(angles) * MSCALE
    sine_part = jnp.sin(angles) * MSCALE
    return jnp.concatenate(
        [front_half * cosine - back_half * sine_part, back_half * cosine + front_half * sine_part],
        axis=-1,
    )


def pick_row(array, where_at):
    return lax.dynamic_index_in_dim(array, where_at, 0, keepdims=False)


def put_row(array, update, where_at):
    return lax.dynamic_update_index_in_dim(array, update, where_at, 0)


def local(features, gain, w_qkv, rope_factors, cache_len, cache_kv, block_owner, block_base):
    local_rows = features.shape[0]
    wide_x = lax.all_gather(features, "tensor", axis=1, tiled=True).astype(jnp.float32)
    normed = (
        wide_x * lax.rsqrt(jnp.mean(wide_x * wide_x, axis=1, keepdims=True) + EPSILON) * gain
    ).astype(jnp.bfloat16)
    projected = jnp.einsum("td,dcf->tcf", normed, w_qkv, preferred_element_type=jnp.float32)
    feat_width = projected.shape[2]
    head_dim = 2 * rope_factors.shape[0]
    head_count = feat_width // head_dim
    requests = cache_len.shape[0]
    seq_count = lax.axis_size("seq")
    all_rows = local_rows * seq_count
    new_len = all_rows // requests
    first_row = lax.axis_index("seq") * local_rows
    request = first_row // new_len
    own_length = pick_row(cache_len, request)
    positions = own_length + first_row % new_len + jnp.arange(local_rows, dtype=jnp.int32)
    inv_freq = 1.0 / (
        rope_factors
        * jnp.power(10000.0, jnp.arange(rope_factors.shape[0], dtype=jnp.float32) * 2.0 / head_dim)
    )
    angles = positions.astype(jnp.float32)[:, None, None] * inv_freq[None, None, :]
    shaped = projected.reshape(local_rows, 3, head_count, head_dim)
    queries = (rotate(shaped[:, 0], angles) * head_dim ** (-0.5)).astype(jnp.bfloat16)
    new_keys = rotate(shaped[:, 1], angles).astype(jnp.bfloat16)
    new_values = shaped[:, 2].astype(jnp.bfloat16)
    new_kv = jnp.stack(
        [new_keys.reshape(local_rows, feat_width), new_values.reshape(local_rows, feat_width)],
        axis=1,
    )
    block_count = cache_kv.shape[0]
    block_len = cache_kv.shape[1]
    slot_steps = jnp.arange(block_len, dtype=jnp.int32)
    cache_keys = cache_kv[:, :, 0].reshape(block_count, block_len, head_count, head_dim)
    cache_values = cache_kv[:, :, 1].reshape(block_count, block_len, head_count, head_dim)
    gathered = lax.all_gather(
        queries.reshape(local_rows, feat_width), "seq", axis=0, tiled=True
    ).reshape(requests, new_len, head_count, head_dim)
    own_queries = pick_row(gathered, request)
    own_pos = own_length + jnp.arange(new_len, dtype=jnp.int32)
    new_scores = jnp.einsum(
        "nhd,khd->hnk", own_queries, new_keys, preferred_element_type=jnp.float32
    )
    new_mask = (positions[None, :] <= own_pos[:, None])[None]

    def block_meta(slot_index):
        owner_id = block_owner[slot_index]
        clamped = jnp.minimum(owner_id, requests - 1)
        bound_len = jnp.where(owner_id < requests, cache_len[clamped], 0)
        usable = (block_base[slot_index] + slot_steps < bound_len)[None, None, :]
        return (usable, clamped)

    def block_scores(slot_index):
        usable, clamped = block_meta(slot_index)
        scores = jnp.einsum(
            "nhd,khd->hnk",
            pick_row(gathered, clamped),
            cache_keys[slot_index],
            preferred_element_type=jnp.float32,
        )
        return (scores, usable, clamped)

    def raise_peak(maxima, scores, usable, clamped):
        block_max = jnp.max(jnp.where(usable, scores, NEGATIVE), axis=2).T
        return put_row(maxima, jnp.maximum(pick_row(maxima, clamped), block_max), clamped)

    maxima = jnp.full((requests, new_len, head_count), NEGATIVE, jnp.float32)
    maxima = raise_peak(maxima, new_scores, new_mask, request)

    def first_loop(slot_index, running):
        scores, usable, clamped = block_scores(slot_index)
        return raise_peak(running, scores, usable, clamped)

    maxima = lax.fori_loop(0, block_count, first_loop, maxima)
    maxima = lax.pmax(maxima, "seq")

    def accumulate(totals, scores, usable, clamped, block_values):
        numerator, denominator = totals
        ceiling = pick_row(maxima, clamped).T[:, :, None]
        weight = jnp.where(usable, jnp.exp(scores - ceiling), 0.0)
        term = jnp.einsum(
            "hnk,khd->nhd",
            weight.astype(jnp.bfloat16),
            block_values,
            preferred_element_type=jnp.float32,
        )
        numerator = put_row(numerator, pick_row(numerator, clamped) + term, clamped)
        denominator = put_row(
            denominator, pick_row(denominator, clamped) + jnp.sum(weight, axis=2).T, clamped
        )
        return (numerator, denominator)

    totals = (
        jnp.zeros((requests, new_len, head_count, head_dim), jnp.float32),
        jnp.zeros((requests, new_len, head_count), jnp.float32),
    )
    totals = accumulate(totals, new_scores, new_mask, request, new_values)

    def second_loop(slot_index, running):
        scores, usable, clamped = block_scores(slot_index)
        return accumulate(running, scores, usable, clamped, cache_values[slot_index])

    totals = lax.fori_loop(0, block_count, second_loop, totals)
    num_all = totals[0].reshape(all_rows, feat_width)
    den_all = totals[1].reshape(all_rows, head_count)
    num_rows, den_rows = (
        lax.psum_scatter(num_all, "seq", scatter_dimension=0, tiled=True),
        lax.psum_scatter(den_all, "seq", scatter_dimension=0, tiled=True),
    )
    attended = num_rows.reshape(local_rows, head_count, head_dim) / den_rows[:, :, None]
    return (attended.reshape(local_rows, feat_width).astype(jnp.bfloat16), new_kv)


def solution(mesh):
    in_specs = (
        P("seq", "tensor"),
        P(),
        P(None, None, "tensor"),
        P(),
        P(),
        P("seq", None, None, "tensor"),
        P("seq"),
        P("seq"),
    )
    out_specs = (P("seq", "tensor"), P("seq", None, "tensor"))
    return jax.shard_map(local, mesh=mesh, in_specs=in_specs, out_specs=out_specs, check_vma=False)
```

profile of v0, /device:TPU:0, one launch (start us, length us, event | category | flops | bytes accessed | tf_op | source)
XLA Modules:
  0.0 677.3 jit_solution(9437656305576258712)
XLA Ops:
  9.8 13.0 %all_gather.6 = bf16[128,3072]{1,0:T(8,128)(2,1)S(1)} all-gather(bf16[128,1536]{1,0:T(8,128)(2,1)} %param.12), channel_id=1, replica_groups=mesh['seq'=16,'tensor'=2] {'tensor'}, dimensions={1}, use_global_device_ids=true | all-gather | bytes 1179648 | tf_op jit(solution)/shard_map/all_gather | solution.py:33
  23.0 15.2 %fusion.46 = f32[128,3,1536]{0,2,1:T(8,128)S(1)} fusion(bf16[3072,3,1536]{2,0,1:T(8,128)(2,1)} %param.14, bf16[128,3072]{1,0:T(8,128)(2,1)S(1)} %all_gather.6, f32[3072]{0:T(1024)} %param.13, f32[128]{0:T(128)S(1)} %add_rsqrt_fusion), kind=kOutput, calls=%fused_computation.57 | convolution fusion | flops 3625451520 | bytes 31470080 | tf_op jit(solution)/shard_map/td,dcf->tcf/dot_general | solution.py:37
  39.7 19.9 %fusion.57 = (bf16[12,128,1,1536]{3,2,1,0:T(2,128)(2,1)}, bf16[12,128,1,1536]{3,2,1,0:T(2,128)(2,1)}) fusion(bf16[12,128,2,1536]{3,2,1,0:T(2,128)(2,1)} %param.17), kind=kLoop, calls=%fused_computation.89 | loop fusion | bytes 18874368 | tf_op jit(solution)/shard_map/slice | solution.py:66
  59.7 22.3 %copy.34 = bf16[12,128,1,1536]{1,3,0,2:T(8,128)(2,1)} copy(bf16[12,128,1,1536]{3,2,1,0:T(2,128)(2,1)} %get-tuple-element.442) | data formatting | bytes 9437184 | tf_op jit(solution)/shard_map/slice | solution.py:65
  84.2 22.5 %all-gather.2.cloned.1.call-done = bf16[2048,1536]{0,1:T(8,128)(2,1)} async-done(((bf16[128,1536]{0,1:T(8,128)(2,1)}), bf16[2048,1536]{0,1:T(8,128)(2,1)}) %all-gather.2.cloned.1.call-update) | async-done | bytes 6291472 | tf_op jit(solution)/shard_map/all_gather | solution.py:67
  106.8 11.2 %reshape.182 = bf16[4,512,16,96]{1,0,3,2:T(4,128)(2,1)} reshape(bf16[2048,1536]{0,1:T(8,128)(2,1)} %all-gather.2.cloned.1.call-done) | data formatting | bytes 12582912 | tf_op jit(solution)/shard_map/reshape | solution.py:69
  117.9 6.6 constant_dynamic-slice_fusion.3
  124.6 4.2 copy.35
  128.8 2.9 select_reduce_fusion.1
  131.7 81.3 %while.30 = (s32[]{:T(128)}, f32[4,512,16]{1,2,0:T(8,128)S(1)}, s32[12]{0:T(128)S(1)}, s32[12]{0:T(128)S(1)}, s32[4]{0:T(128)S(1)}, /*index=5*/bf16[4,512,16,96]...) while((s32[]{:T(128)}, f32[4,512,16]{1,2,0:T(8,128)S(1)}, ...), condition=%wide.region_4.5_spmd.clone, body=%wide.region_2.4_spmd.clone.sunk | while | flops 203424000 | bytes 2163205 | solution.py:105
  136.1 2.3 select_reduce_fusion.3
  142.9 2.3 select_reduce_fusion.3
  149.7 2.3 select_reduce_fusion.3
  156.4 2.3 select_reduce_fusion.3
  163.2 2.3 select_reduce_fusion.3
  170.0 2.3 select_reduce_fusion.3
  176.8 2.3 select_reduce_fusion.3
  183.5 2.3 select_reduce_fusion.3
  190.3 2.3 select_reduce_fusion.3
  197.1 2.3 select_reduce_fusion.3
  203.9 2.3 select_reduce_fusion.3
  210.7 2.3 select_reduce_fusion.3
  214.0 22.2 %copy.37 = bf16[12,128,1,1536]{1,3,0,2:T(8,128)(2,1)} copy(bf16[12,128,1,1536]{3,2,1,0:T(2,128)(2,1)} %get-tuple-element.441) | data formatting | bytes 9437184 | tf_op jit(solution)/shard_map/slice | solution.py:66
  236.2 62.9 %all-reduce.2.cloned.1.call-done = f32[4,512,16]{1,2,0:T(8,128)} async-done(((f32[4,512,16]{1,2,0:T(8,128)}), f32[4,512,16]{1,2,0:T(8,128)}) %all-reduce.2.cloned.1.call-update) | async-done | bytes 131088 | tf_op jit(solution)/shard_map/pmax | solution.py:106
  299.9 2.9 fusion.30
  305.9 4.5 copy-done
  310.4 165.3 %while.31 = (s32[]{:T(128)}, f32[4,512,16,96]{1,3,2,0:T(8,128)}, f32[4,512,16]{1,2,0:T(8,128)S(1)}, s32[12]{0:T(128)S(1)}, bf16[12,128,16,96]{1,3,2,0:T(8,128)(2...) while((s32[]{:T(128)}, f32[4,512,16,96]{1,3,2,0:T(8,128)}, ...), condition=%wide.region_9.10_spmd.clone, body=%wide.region_7.9_spmd.clone.sunk | while | flops 409731328 | bytes 23659180 | solution.py:134
  315.5 2.3 constant_dynamic-slice_fusion.8
  317.8 2.7 fusion.73
  320.5 3.6 bitcast_dynamic-update-slice_fusion.10
  329.3 2.3 constant_dynamic-slice_fusion.8
  331.6 2.7 fusion.73
  334.3 3.6 bitcast_dynamic-update-slice_fusion.10
  343.0 2.3 constant_dynamic-slice_fusion.8
  345.3 2.7 fusion.73
  348.0 3.6 bitcast_dynamic-update-slice_fusion.10
  356.8 2.3 constant_dynamic-slice_fusion.8
  359.0 2.7 fusion.73
  361.7 3.6 bitcast_dynamic-update-slice_fusion.10
  370.5 2.3 constant_dynamic-slice_fusion.8
  372.7 2.7 fusion.73
  375.4 3.6 bitcast_dynamic-update-slice_fusion.10
  384.2 2.3 constant_dynamic-slice_fusion.8
  386.5 2.7 fusion.73
  389.2 3.7 bitcast_dynamic-update-slice_fusion.10
  398.0 2.3 constant_dynamic-slice_fusion.8
  400.3 2.7 fusion.73
  403.0 3.7 bitcast_dynamic-update-slice_fusion.10
  411.8 2.3 constant_dynamic-slice_fusion.8
  414.1 2.7 fusion.73
  416.8 3.7 bitcast_dynamic-update-slice_fusion.10
  427.9 2.7 fusion.73
  430.6 3.6 bitcast_dynamic-update-slice_fusion.10
  441.6 2.7 fusion.73
  444.3 3.7 bitcast_dynamic-update-slice_fusion.10
  455.5 2.7 fusion.73
  458.1 3.8 bitcast_dynamic-update-slice_fusion.10
  469.3 2.7 fusion.73
  472.0 3.7 bitcast_dynamic-update-slice_fusion.10
  476.5 16.4 %copy.39 = f32[4,512,16,96]{1,0,3,2:T(4,128)} copy(f32[4,512,16,96]{1,3,2,0:T(8,128)} %get-tuple-element.327) | data formatting | bytes 25165824 | tf_op jit(solution)/shard_map/while | solution.py:134
  492.9 15.4 %copy.49 = f32[192,8,4,512]{3,1,2,0:T(8,128)} copy(f32[192,8,4,512]{3,2,1,0:T(4,128)} %bitcast.148) | data formatting | bytes 25165824
  509.9 2.7 pad_maximum_fusion
  512.5 17.8 %reduce-scatter.5.cloned.1.call-done = f32[128,16]{0,1:T(8,128)} async-done(((f32[2048,16]{0,1:T(8,128)}), f32[128,16]{0,1:T(8,128)}) %reduce-scatter.5.cloned.1.call-update) | async-done | bytes 8208 | tf_op jit(solution)/shard_map/reduce_scatter | solution.py:139
  530.4 138.3 %reduce-scatter.3.cloned.1.call-done = f32[128,1536]{0,1:T(8,128)} async-done(((f32[2048,1536]{0,1:T(8,128)}), f32[128,1536]{0,1:T(8,128)}) %reduce-scatter.3.cloned.1.call-update) | async-done | bytes 786448 | tf_op jit(solution)/shard_map/reduce_scatter | solution.py:138
  (214 shorter events, 91.6 us)
Async XLA Ops:
  7.2 99.6 %all-gather.2.cloned.1.call-start = ((), (), s32[]{:S(2)}) async-start(), calls=%async_computation.2 | async-start | bytes 6684672 | tf_op jit(solution)/shard_map/all_gather | solution.py:67
  38.5 0.9 copy-start.5
  38.5 0.9 copy-start.6
  39.5 259.6 %all-reduce.2.cloned.1.call-start = ((), (), s32[]{:S(2)}) async-start(), calls=%async_computation.3 | async-start | bytes 262144 | tf_op jit(solution)/shard_map/pmax | solution.py:106
  117.9 6.6 copy-start.1
  124.6 4.2 copy-start.4
  128.8 2.9 copy-start.7
  128.8 2.9 copy-start.8
  128.8 2.9 copy-start.9
  213.1 0.7 copy-start.3
  213.7 316.6 %reduce-scatter.5.cloned.1.call-start = ((), (), s32[]{:S(2)}) async-start(), calls=%async_computation.5 | async-start | bytes 139264 | tf_op jit(solution)/shard_map/reduce_scatter | solution.py:139
  302.8 2.2 copy-start.2
  305.9 4.5 copy-start
  476.4 192.2 %reduce-scatter.3.cloned.1.call-start = ((), (), s32[]{:S(2)}) async-start(), calls=%async_computation.4 | async-start | bytes 13369344 | tf_op jit(solution)/shard_map/reduce_scatter | solution.py:138
Sparse Core Ops, SparseCore 0:
  39.6 67.1 all-gather.1
  213.9 85.2 all-reduce.1
  476.5 53.8 reduce-scatter.4
  534.8 133.7 reduce-scatter.2
where the time goes:
time: 683 us; the launch traced here: 677 us
  waiting for transfers between devices  242 us (35%)
  local copies, waits for them, and re-layouts  210 us (31%)
  matrix products  123 us (18%)
  loops' own time  47.9 us (7%)
  other arithmetic  26.9 us (4%)
  between operations  14.7 us (2%)
  blocking collectives  13 us (2%)
    reduce_scatter x1, waiting for transfers between devices, local(): lax.psum_scatter(num_all, 'seq', scatter_dimension=0, tiled=True)  138 us
    pmax x1, waiting for transfers between devices, local(): maxima = lax.pmax(maxima, 'seq')  62.9 us
    dot_general x24, matrix products, block_scores(): jnp.einsum('nhd,khd->hnk', pick_row(gathered, clamped), cache_keys[slot_i...  60.1 us
    dot_general x13, matrix products, accumulate(): jnp.einsum('hnk,khd->nhd', weight.astype(jnp.bfloat16), block_values, pre...  45 us
    slice x2, local copies, waits for them, and re-layouts, local(): cache_kv[:, :, 1].reshape(block_count, block_len, head_count, head_dim)  42.2 us
    dynamic_slice x38, local copies, waits for them, and re-layouts, pick_row(): return lax.dynamic_index_in_dim(array, where_at, 0, keepdims=False)  35 us
    unnamed x23, local copies, waits for them, and re-layouts  26.3 us
    another operation x1, loops' own time, local(): maxima = lax.fori_loop(0, block_count, first_loop, maxima)  24 us
  transfers between devices with their start and end apart: 4, of which 4 were waited for; matrix products, arithmetic and copies ran while one was open for 15% of the time, Pallas kernels for 0%

commit v1 on v0

v1 whole, which is shorter than its diff:
```python
import functools
import jax
import jax.numpy as jnp
from jax import lax
from jax.experimental import pallas as pl
from jax.experimental.pallas import tpu as pltpu
from jax.sharding import PartitionSpec as P

EPSILON = 1e-05
FLOOR = -1e30
MASKED = -2e30
MSCALE = 1.1902380714238083
GROUP = 4


def rotate_rows(vectors, cosine, sine):
    half = vectors.shape[1] // 2
    front, back = vectors[:, :half], vectors[:, half:]
    return jnp.concatenate([front * cosine - back * sine, back * cosine + front * sine], axis=1)


def attend_kernel(
    owner_ref, bound_ref, place_ref, first_ref,
    q_ref, k_ref, v_ref, nk_ref, nv_ref, out_ref, stat_ref, acc, peak, total,
    *, requests, per_request, head_dim,
):
    rows = q_ref.shape[2]
    blocks, slots = k_ref.shape[0], k_ref.shape[1]
    width = per_request * rows
    acc[...] = jnp.zeros_like(acc)
    peak[...] = jnp.full_like(peak, FLOOR)
    total[...] = jnp.zeros_like(total)

    def step(request, keys, values, mask):
        for head in range(GROUP):
            span = slice(head * head_dim, (head + 1) * head_dim)
            queries = jnp.concatenate(
                [q_ref[request * per_request + c, span, :] for c in range(per_request)], axis=1
            )
            scores = jnp.dot(keys[:, span], queries, preferred_element_type=jnp.float32)
            scores = jnp.where(mask, scores, MASKED)
            old = peak[request, head : head + 1, :]
            new = jnp.maximum(old, jnp.max(scores, axis=0, keepdims=True))
            weight = jnp.exp(scores - new)
            fade = jnp.exp(old - new)
            peak[request, head : head + 1, :] = new
            total[request, head : head + 1, :] = total[request, head : head + 1, :] * fade + jnp.sum(
                weight, axis=0, keepdims=True
            )
            term = lax.dot_general(
                values[:, span], weight.astype(jnp.bfloat16), (((0,), (0,)), ((), ())),
                preferred_element_type=jnp.float32,
            )
            acc[request, span, :] = acc[request, span, :] * fade + term

    own_rows = nk_ref.shape[0]
    key_at = lax.broadcasted_iota(jnp.int32, (own_rows, width), 0) + first_ref[1]
    query_at = lax.broadcasted_iota(jnp.int32, (own_rows, width), 1)
    step(first_ref[0], nk_ref[...], nv_ref[...], key_at <= query_at)

    slot_at = lax.broadcasted_iota(jnp.int32, (slots, width), 0)

    def one_block(block, carry):
        @pl.when(bound_ref[block] > 0)
        def _():
            step(owner_ref[block], k_ref[block], v_ref[block], slot_at < bound_ref[block])

        return carry

    lax.fori_loop(0, blocks, one_block, 0)

    for request in range(requests):
        for c in range(per_request):
            chunk = slice(c * rows, (c + 1) * rows)
            where_to = place_ref[request * per_request + c]
            out_ref[where_to] = acc[request, :, chunk].astype(jnp.bfloat16)
            stat_ref[where_to, 0] = jnp.concatenate(
                [peak[request, :, chunk], total[request, :, chunk]], axis=0
            )


def attend(owner, bound, place, first, queries, keys, values, new_keys, new_values, requests, head_dim):
    seq, feats, rows = queries.shape
    blocks, slots = keys.shape[:2]
    span = GROUP * head_dim
    groups = feats // span
    per_request = seq // requests
    own_rows = new_keys.shape[0]
    width = per_request * rows
    work = (blocks + 1) * slots * width * feats * 4
    return pl.pallas_call(
        functools.partial(
            attend_kernel, requests=requests, per_request=per_request, head_dim=head_dim
        ),
        grid_spec=pltpu.PrefetchScalarGridSpec(
            num_scalar_prefetch=4,
            grid=(groups,),
            in_specs=[
                pl.BlockSpec((seq, span, rows), lambda g, *_: (0, g, 0)),
                pl.BlockSpec((blocks, slots, span), lambda g, *_: (0, 0, g)),
                pl.BlockSpec((blocks, slots, span), lambda g, *_: (0, 0, g)),
                pl.BlockSpec((own_rows, span), lambda g, *_: (0, g)),
                pl.BlockSpec((own_rows, span), lambda g, *_: (0, g)),
            ],
            out_specs=[
                pl.BlockSpec((seq, span, rows), lambda g, *_: (0, g, 0)),
                pl.BlockSpec((seq, 1, 2 * GROUP, rows), lambda g, *_: (0, g, 0, 0)),
            ],
            scratch_shapes=[
                pltpu.VMEM((requests, span, width), jnp.float32),
                pltpu.VMEM((requests, GROUP, width), jnp.float32),
                pltpu.VMEM((requests, GROUP, width), jnp.float32),
            ],
        ),
        out_shape=[
            jax.ShapeDtypeStruct((seq, feats, rows), jnp.bfloat16),
            jax.ShapeDtypeStruct((seq, groups, 2 * GROUP, rows), jnp.float32),
        ],
        compiler_params=pltpu.CompilerParams(vmem_limit_bytes=48 * 1024 * 1024),
        cost_estimate=pl.CostEstimate(
            flops=8 * work, bytes_accessed=4 * queries.size + 4 * keys.size,
            transcendentals=work // (4 * head_dim),
        ),
    )(owner, bound, place, first, queries, keys, values, new_keys, new_values)


def merge(part_a, part_b, head_dim):
    out_a, stat_a = part_a
    out_b, stat_b = part_b
    count, groups, _, rows = stat_a.shape
    peak_a, peak_b = stat_a[:, :, :GROUP], stat_b[:, :, :GROUP]
    top = jnp.maximum(peak_a, peak_b)
    fade_a, fade_b = jnp.exp(peak_a - top), jnp.exp(peak_b - top)
    total = stat_a[:, :, GROUP:] * fade_a + stat_b[:, :, GROUP:] * fade_b
    shape = (count, groups, GROUP, head_dim, rows)
    out = (
        out_a.reshape(shape).astype(jnp.float32) * fade_a[:, :, :, None]
        + out_b.reshape(shape).astype(jnp.float32) * fade_b[:, :, :, None]
    )
    return out, top, total


def reduce_halves(out, stat, seq, head_dim):
    bit = 1
    while bit < seq:
        half = out.shape[0] // 2
        swap = [(i, i ^ bit) for i in range(seq)]
        came_out = lax.ppermute(out[half:], "seq", swap)
        came_stat = lax.ppermute(stat[half:], "seq", swap)
        merged, top, total = merge((out[:half], stat[:half]), (came_out, came_stat), head_dim)
        bit *= 2
        if bit < seq:
            out = merged.astype(jnp.bfloat16).reshape((half,) + out.shape[1:])
            stat = jnp.concatenate([top, total], axis=2)
    return merged[0] / total[0][:, :, None]


def local(features, gain, w_qkv, rope_factors, cache_len, cache_kv, block_owner, block_base):
    rows = features.shape[0]
    seq = lax.axis_size("seq")
    me = lax.axis_index("seq")
    wide_x = lax.all_gather(features, "tensor", axis=1, tiled=True).astype(jnp.float32)
    normed = (
        wide_x * lax.rsqrt(jnp.mean(wide_x * wide_x, axis=1, keepdims=True) + EPSILON) * gain
    ).astype(jnp.bfloat16)
    projected = jnp.einsum("td,dcf->cft", normed, w_qkv, preferred_element_type=jnp.float32)
    feats = projected.shape[1]
    head_dim = 2 * rope_factors.shape[0]
    heads = feats // head_dim
    requests = cache_len.shape[0]
    per_request = seq // requests
    request = me // per_request
    first_row = (me % per_request) * rows
    positions = cache_len[request] + first_row + jnp.arange(rows, dtype=jnp.int32)
    inv_freq = 1.0 / (
        rope_factors
        * jnp.power(10000.0, jnp.arange(rope_factors.shape[0], dtype=jnp.float32) * 2.0 / head_dim)
    )
    angles = inv_freq[None, :, None] * positions.astype(jnp.float32)[None, None, :]
    cosine, sine = jnp.cos(angles) * MSCALE, jnp.sin(angles) * MSCALE
    shaped = projected.reshape(3, heads, head_dim, rows)
    queries = (rotate_rows(shaped[0], cosine, sine) * head_dim ** (-0.5)).astype(jnp.bfloat16)
    new_keys = rotate_rows(shaped[1], cosine, sine).astype(jnp.bfloat16).reshape(feats, rows).T
    new_values = shaped[2].astype(jnp.bfloat16).reshape(feats, rows).T
    new_kv = jnp.stack([new_keys, new_values], axis=1)

    clamped = jnp.minimum(block_owner, requests - 1)
    bound = jnp.where(block_owner < requests, cache_len[clamped] - block_base, 0)
    place = jnp.zeros((seq,), jnp.int32)
    flipped = jnp.arange(seq, dtype=jnp.int32) ^ me
    bit = 1
    while bit < seq:
        place = place * 2 + (flipped // bit) % 2
        bit *= 2
    first = jnp.stack([request, first_row]).astype(jnp.int32)
    cache_keys, cache_values = cache_kv[:, :, 0], cache_kv[:, :, 1]
    queries = queries.reshape(feats, rows)

    groups = heads // GROUP
    parts = 2 if groups % 2 == 0 else 1
    wide = feats // parts
    gathered = [
        lax.all_gather(queries[i * wide : (i + 1) * wide], "seq", axis=0) for i in range(parts)
    ]
    results = []
    for i in range(parts):
        cols = slice(i * wide, (i + 1) * wide)
        out, stat = attend(
            clamped, bound, place, first, gathered[i],
            cache_keys[:, :, cols], cache_values[:, :, cols],
            new_keys[:, cols], new_values[:, cols], requests, head_dim,
        )
        results.append(reduce_halves(out, stat, seq, head_dim).reshape(wide, rows))
    attended = jnp.concatenate(results, axis=0).astype(jnp.bfloat16).T
    return (attended, new_kv)


def solution(mesh):
    in_specs = (
        P("seq", "tensor"),
        P(),
        P(None, None, "tensor"),
        P(),
        P(),
        P("seq", None, None, "tensor"),
        P("seq"),
        P("seq"),
    )
    out_specs = (P("seq", "tensor"), P("seq", None, "tensor"))
    return jax.shard_map(local, mesh=mesh, in_specs=in_specs, out_specs=out_specs, check_vma=False)
```

time: 683 us -> 245 us (0.36)
  waiting for transfers between devices: 242 us -> 73.5 us
  local copies, waits for them, and re-layouts: 210 us -> 57.3 us
  matrix products: 123 us -> 11.2 us
  Pallas kernels: 0 us -> 49 us
  loops' own time: 47.9 us -> 0 us
  other arithmetic: 26.9 us -> 7.03 us
  starting transfers between devices: 0.56 us -> 18.1 us
    reduce_scatter x2 -> x0, waiting for transfers between devices: 156 us -> none  [the longest x1 138 us: local(): lax.psum_scatter(num_all, 'seq', scatter_dimension=0, tiled=True)]
    dot_general x39 -> x1, matrix products: 123 us -> 11.2 us  [local(): jnp.einsum('td,dcf->cft', normed, w_qkv, preferred_element_type=jnp.float32)]
    dynamic_slice x110 -> x1, local copies, waits for them, and re-layouts: 77.4 us -> 1.24 us  [local(): cache_len[request] + first_row + jnp.arange(rows, dtype=jnp.int32)]
    pmax x1 -> x0, waiting for transfers between devices: 62.9 us -> none  [local(): maxima = lax.pmax(maxima, 'seq')]
    ppermute x0 -> x16, waiting for transfers between devices: none -> 53.2 us  [the longest x8 47.8 us: reduce_halves(): came_out = lax.ppermute(out[half:], 'seq', swap)]
    pallas_call x0 -> x2, Pallas kernels: none -> 49 us  [attend(): pl.pallas_call(functools.partial(attend_kernel, requests=requests, per_re...]
    another operation x2 -> x0, loops' own time: 47.9 us -> none  [the longest x1 24 us: local(): maxima = lax.fori_loop(0, block_count, first_loop, maxima)]
    slice x4 -> x18, local copies, waits for them, and re-layouts: 64.6 us -> 36.9 us  [the longest x1 20 us: local(): cache_keys, cache_values = (cache_kv[:, :, 0], cache_kv[:, :, 1])]
  transfers between devices with their start and end apart: 4 -> 18, of which waited for: 4 -> 9; matrix products, arithmetic and copies ran while one was open for 15% -> 20% of each run, Pallas kernels for 0% -> 20%
where the time goes in v1:
time: 245 us; the launch traced here: 244 us
  waiting for transfers between devices  73.5 us (30%)
  local copies, waits for them, and re-layouts  57.3 us (23%)
  Pallas kernels  49 us (20%)
  starting transfers between devices  18.1 us (7%)
  between operations  15.1 us (6%)
  blocking collectives  13 us (5%)
  matrix products  11.2 us (5%)
  other arithmetic  7.03 us (3%)
    pallas_call x2, Pallas kernels, attend(): pl.pallas_call(functools.partial(attend_kernel, requests=requests, per_re...  49 us
    ppermute x8, waiting for transfers between devices, reduce_halves(): came_out = lax.ppermute(out[half:], 'seq', swap)  47.8 us
    slice x1, local copies, waits for them, and re-layouts, local(): cache_keys, cache_values = (cache_kv[:, :, 0], cache_kv[:, :, 1])  20 us
    all_gather x2, waiting for transfers between devices, local(): lax.all_gather(queries[i * wide:(i + 1) * wide], 'seq', axis=0)  19.8 us
    all_gather x1, blocking collectives, local(): lax.all_gather(features, 'tensor', axis=1, tiled=True).astype(jnp.float32)  13 us
    ppermute x8, starting transfers between devices, reduce_halves(): came_stat = lax.ppermute(stat[half:], 'seq', swap)  11.8 us
    dot_general x1, matrix products, local(): jnp.einsum('td,dcf->cft', normed, w_qkv, preferred_element_type=jnp.float32)  11.2 us
    squeeze x1, local copies, waits for them, and re-layouts, local(): cache_keys, cache_values = (cache_kv[:, :, 0], cache_kv[:, :, 1])  10.7 us
  transfers between devices with their start and end apart: 18, of which 9 were waited for; matrix products, arithmetic and copies ran while one was open for 20% of the time, Pallas kernels for 20%

profile of v1, /device:TPU:0, one launch (start us, length us, event | category | flops | bytes accessed | tf_op | source)
XLA Modules:
  0.0 244.2 jit_solution(6510510895396006709)
XLA Ops:
  7.2 1.2 dynamic_slice.3
  9.1 0.7 multiply_divide_fusion
  9.8 13.0 %all_gather.15 = bf16[128,3072]{1,0:T(8,128)(2,1)S(1)} all-gather(bf16[128,1536]{1,0:T(8,128)(2,1)} %param.8), channel_id=1, replica_groups=mesh['seq'=16,'tensor'=2] {'tensor'}, dimensions={1}, use_global_device_ids=true | all-gather | bytes 1179648 | tf_op jit(solution)/shard_map/all_gather | solution.py:162
  22.8 0.2 fusion.4
  23.0 11.2 %convolution_bitcast_fusion = f32[3,1536,128]{1,2,0:T(8,128)S(1)} fusion(bf16[3072,3,1536]{2,0,1:T(8,128)(2,1)} %param.10, bf16[128,3072]{1,0:T(8,128)(2,1)S(1)} %all_gather.15, f32[3072]{0:T(1024)} %param.9, f32[128]{0:T(128)S(1)} %add_rsqrt_fusion), kind=kOutput, calls=%fused_computation.11 | convolution fusion | flops 3625451520 | bytes 31470080 | tf_op jit(solution)/shard_map/td,dcf->cft/dot_general | solution.py:166
  34.2 1.3 fusion.59
  35.5 1.4 copy.26
  36.9 2.3 copy.29
  39.2 0.2 fusion.28
  39.3 1.3 subtract_convert_fusion
  40.7 0.1 fusion.13
  40.8 0.8 fusion.62
  41.6 0.2 all-gather.5.cloned.1.call-start
  41.8 0.5 all-gather.5.cloned.1.call-update
  42.4 0.2 copy.30
  42.6 20.0 %fusion.54 = (bf16[12,128,1,1536]{3,2,1,0:T(2,128)(2,1)}, bf16[12,128,1,1536]{3,2,1,0:T(2,128)(2,1)}) fusion(bf16[12,128,2,1536]{3,2,1,0:T(2,128)(2,1)} %param.13), kind=kLoop, calls=%fused_computation.154 | loop fusion | bytes 18874368 | tf_op jit(solution)/shard_map/slice | solution.py:196
  62.6 0.7 gather_fusion
  63.3 0.1 pad_maximum_fusion
  63.4 1.7 copy.32
  65.1 0.1 pad_add_fusion.first_ref
  65.3 10.7 %copy_bitcast_fusion = (bf16[12,128,1536]{2,1,0:T(8,128)(2,1)S(1)}, bf16[12,128,1536]{2,1,0:T(8,128)(2,1)S(1)}) fusion(bf16[12,128,1,1536]{3,2,1,0:T(2,128)(2,1)} %get-tuple-element.40, bf16[12,128,1,1536]{3,2,1,0:T(2,128)(2,1)} %get-tuple-element.41), kind=kLoop, calls=%fused_computation.1 | loop fusion | bytes 18874368 | tf_op jit(solution)/shard_map/squeeze | solution.py:196
  76.0 2.0 fusion.55
  78.0 2.7 %fusion.56 = (bf16[12,128,768]{2,1,0:T(8,128)(2,1)}, bf16[12,128,768]{2,1,0:T(8,128)(2,1)}) fusion(bf16[12,128,1536]{2,1,0:T(8,128)(2,1)S(1)} %get-tuple-element.77), kind=kLoop, calls=%fused_computation.156 | loop fusion | bytes 9437184 | tf_op jit(solution)/shard_map/slice | solution.py:210
  80.7 7.7 %all-gather.3.cloned.1.call-done.q_ref = bf16[16,768,128]{2,1,0:T(8,128)(2,1)} async-done(((bf16[1,768,128]{2,1,0:T(8,128)(2,1)}), bf16[16,768,128]{2,1,0:T(8,128)(2,1)}) %all-gather.3.cloned.1.call-update) | async-done | bytes 3145744 | tf_op jit(solution)/shard_map/all_gather | solution.py:203
  88.4 1.7 copy-done.1
  90.0 1.7 copy-done.2
  91.7 24.5 %shard_map.95 = (bf16[16,768,128]{2,1,0:T(8,128)(2,1)}, f32[16,2,8,128]{3,2,1,0:T(8,128)S(1)}) custom-call(s32[12]{0:T(128)S(1)} %get-tuple-element.75.owner_ref, s32[12]{0:T(128)S(1)} %get-tuple-element.74.bound_ref, s32[16]{0:T(128)S(1)} %fusion.44.place_ref, s32[2]{0:T(128)S(1)} %pad_add_fusion.first_ref, ...), custom_call_target="tpu_custom_call" | custom-call | flops 20937965568 | bytes 11010048 | tf_op jit(solution)/shard_map/pallas_call | solution.py:91
  116.2 2.5 %collective-permute-start = (f32[8,2,8,128]{3,2,1,0:T(8,128)S(1)}, f32[8,2,8,128]{3,2,1,0:T(8,128)S(1)}, u32[]{:S(2)}, u32[]{:S(2)}) collective-permute-start(f32[8,2,8,128]{3,2,1,0:T(8,128)S(1)} %slice.307), channel_id=1, source_target_pairs={{0,2},{2,0},{4,6},{6,4},{8,10},{10,8},{12,14},{14,12},{16,18},{18,... | collective-permute-start | bytes 196616 | tf_op jit(solution)/shard_map/ppermute | solution.py:149
  118.7 3.9 %fusion.57 = (bf16[8,768,128]{2,1,0:T(8,128)(2,1)}, bf16[8,768,128]{2,1,0:T(8,128)(2,1)}) fusion(bf16[16,768,128]{2,1,0:T(8,128)(2,1)} %get-tuple-element.6), kind=kLoop, calls=%fused_computation.157 | loop fusion | bytes 6291456 | tf_op jit(solution)/shard_map/slice | solution.py:150
  122.6 12.1 %all-gather.5.cloned.1.call-done.q_ref = bf16[16,768,128]{2,1,0:T(8,128)(2,1)} async-done(((bf16[1,768,128]{2,1,0:T(8,128)(2,1)}), bf16[16,768,128]{2,1,0:T(8,128)(2,1)}) %all-gather.5.cloned.1.call-update) | async-done | bytes 3145744 | tf_op jit(solution)/shard_map/all_gather | solution.py:203
  134.7 1.7 copy-done
  136.4 24.5 %shard_map.96 = (bf16[16,768,128]{2,1,0:T(8,128)(2,1)}, f32[16,2,8,128]{3,2,1,0:T(8,128)S(1)}) custom-call(s32[12]{0:T(128)S(1)} %get-tuple-element.75.owner_ref, s32[12]{0:T(128)S(1)} %get-tuple-element.74.bound_ref, s32[16]{0:T(128)S(1)} %fusion.44.place_ref, s32[2]{0:T(128)S(1)} %pad_add_fusion.first_ref, ...), custom_call_target="tpu_custom_call" | custom-call | flops 20937965568 | bytes 11010048 | tf_op jit(solution)/shard_map/pallas_call | solution.py:91
  160.9 2.5 %collective-permute-start.8 = (f32[8,2,8,128]{3,2,1,0:T(8,128)S(1)}, f32[8,2,8,128]{3,2,1,0:T(8,128)S(1)}, u32[]{:S(2)}, u32[]{:S(2)}) collective-permute-start(f32[8,2,8,128]{3,2,1,0:T(8,128)S(1)} %slice.343), channel_id=1, source_target_pairs={{0,2},{2,0},{4,6},{6,4},{8,10},{10,8},{12,14},{14,12},{16,18},{18,... | collective-permute-start | bytes 196616 | tf_op jit(solution)/shard_map/ppermute | solution.py:149
  163.4 2.3 fusion.58
  165.7 0.1 collective-permute-start.9
  165.9 3.1 %collective-permute-start.2 = (f32[4,2,8,128]{3,2,1,0:T(8,128)S(1)}, f32[4,2,8,128]{3,2,1,0:T(8,128)S(1)}, u32[]{:S(2)}, u32[]{:S(2)}) collective-permute-start(f32[4,2,8,128]{3,2,1,0:T(8,128)S(1)} %pad_maximum_fusion.3), channel_id=1, source_target_pairs={{0,4},{2,6},{4,0},{6,2},{8,12},{10,14},{12,8},{14,10},{16,20},{18,... | collective-permute-start | bytes 98312 | tf_op jit(solution)/shard_map/ppermute | solution.py:149
  169.0 0.1 collective-permute-start.10
  169.1 1.7 collective-permute-done.2
  170.9 0.1 collective-permute-start.4
  171.0 2.0 collective-permute-done.10
  173.1 0.1 collective-permute-start.12
  173.1 1.6 collective-permute-done.4
  174.8 3.4 %collective-permute-start.6 = (f32[1,2,8,128]{3,2,1,0:T(8,128)S(1)}, f32[1,2,8,128]{3,2,1,0:T(8,128)S(1)}, u32[]{:S(2)}, u32[]{:S(2)}) collective-permute-start(f32[1,2,8,128]{3,2,1,0:T(8,128)S(1)} %pad_maximum_fusion.7), channel_id=1, source_target_pairs={{0,16},{2,18},{4,20},{6,22},{8,24},{10,26},{12,28},{14,30},{16,0},... | collective-permute-start | bytes 24584 | tf_op jit(solution)/shard_map/ppermute | solution.py:149
  178.2 2.0 fusion.3
  180.3 1.7 collective-permute-start.3
  181.9 0.7 fusion.1
  182.6 0.1 slice.416
  182.7 0.5 collective-permute-start.11
  183.3 0.1 collective-permute-start.14
  183.4 17.4 %collective-permute-done.3 = bf16[4,768,128]{2,1,0:T(8,128)(2,1)S(1)} collective-permute-done((bf16[4,768,128]{2,1,0:T(8,128)(2,1)S(1)}, bf16[4,768,128]{2,1,0:T(8,128)(2,1)S(1)}, u32[]{:S(2)}, u32[]{:S(2)}) %collective-permute-start.3) | collective-permute-done | bytes 786464 | tf_op jit(solution)/shard_map/ppermute | solution.py:148
  200.8 0.4 fusion.10
  201.2 1.7 collective-permute-start.5
  202.8 11.8 %collective-permute-done.11 = bf16[4,768,128]{2,1,0:T(8,128)(2,1)S(1)} collective-permute-done((bf16[4,768,128]{2,1,0:T(8,128)(2,1)S(1)}, bf16[4,768,128]{2,1,0:T(8,128)(2,1)S(1)}, u32[]{:S(2)}, u32[]{:S(2)}) %collective-permute-start.11) | collective-permute-done | bytes 786464 | tf_op jit(solution)/shard_map/ppermute | solution.py:148
  214.7 0.4 fusion.8
  215.1 1.6 collective-permute-start.13
  216.7 0.2 fusion.17
  216.9 0.4 collective-permute-start.7
  217.3 10.2 %collective-permute-done.13 = bf16[2,768,128]{2,1,0:T(8,128)(2,1)S(1)} collective-permute-done((bf16[2,768,128]{2,1,0:T(8,128)(2,1)S(1)}, bf16[2,768,128]{2,1,0:T(8,128)(2,1)S(1)}, u32[]{:S(2)}, u32[]{:S(2)}) %collective-permute-start.13) | collective-permute-done | bytes 393248 | tf_op jit(solution)/shard_map/ppermute | solution.py:148
  227.5 0.2 fusion.15
  227.7 0.1 collective-permute-start.15
  227.8 0.1 fusion.21
  227.9 8.4 %collective-permute-done.15 = bf16[1,768,128]{2,1,0:T(8,128)(2,1)S(1)} collective-permute-done((bf16[1,768,128]{2,1,0:T(8,128)(2,1)S(1)}, bf16[1,768,128]{2,1,0:T(8,128)(2,1)S(1)}, u32[]{:S(2)}, u32[]{:S(2)}) %collective-permute-start.15) | collective-permute-done | bytes 196640 | tf_op jit(solution)/shard_map/ppermute | solution.py:148
  236.3 0.1 fusion.20
  236.4 0.9 copy.31
  (56 shorter events, 0.8 us)
Async XLA Ops:
  7.2 81.2 %all-gather.3.cloned.1.call-start = ((), (), s32[]{:S(2)}) async-start(), calls=%async_computation | async-start | bytes 3342336 | tf_op jit(solution)/shard_map/all_gather | solution.py:203
  41.6 93.1 %all-gather.5.cloned.1.call-start = ((), (), s32[]{:S(2)}) async-start(), calls=%async_computation.1 | async-start | bytes 3342336 | tf_op jit(solution)/shard_map/all_gather | solution.py:203
  42.5 20.0 %copy-start.5 = (s32[12]{0:T(128)S(1)}, s32[12]{0:T(128)}, u32[]{:S(2)}) copy-start(s32[12]{0:T(128)} %param.14) | copy-start | bytes 148
  42.6 20.0 %copy-start.3 = (s32[4]{0:T(128)S(1)}, s32[4]{0:T(128)}, u32[]{:S(2)}) copy-start(s32[4]{0:T(128)} %param.12) | copy-start | bytes 52
  62.6 2.6 %copy-start.6 = (s32[12]{0:T(128)S(1)}, s32[12]{0:T(128)}, u32[]{:S(2)}) copy-start(s32[12]{0:T(128)} %param.15) | copy-start | bytes 148
  88.4 1.7 copy-start.1
  90.0 1.7 copy-start.2
  116.2 49.6 %collective-permute-start = (f32[8,2,8,128]{3,2,1,0:T(8,128)S(1)}, f32[8,2,8,128]{3,2,1,0:T(8,128)S(1)}, u32[]{:S(2)}, u32[]{:S(2)}) collective-permute-start(f32[8,2,8,128]{3,2,1,0:T(8,128)S(1)} %slice.307), channel_id=1, source_target_pairs={{0,2},{2,0},{4,6},{6,4},{8,10},{10,8},{12,14},{14,12},{16,18},{18,... | collective-permute-start | bytes 196616 | tf_op jit(solution)/shard_map/ppermute | solution.py:149
  122.6 55.6 %collective-permute-start.1 = (bf16[8,768,128]{2,1,0:T(8,128)(2,1)}, bf16[8,768,128]{2,1,0:T(8,128)(2,1)}, u32[]{:S(2)}, u32[]{:S(2)}) collective-permute-start(bf16[8,768,128]{2,1,0:T(8,128)(2,1)} %get-tuple-element.47), channel_id=1, source_target_pairs={{0,2},{2,0},{4,6},{6,4},{8,10},{10,8},{12,14},{14,12},{16,18},{18,... | collective-permute-start | bytes 4718600 | tf_op jit(solution)/shard_map/ppermute | solution.py:148
  134.7 1.7 copy-start
  160.9 8.1 %collective-permute-start.8 = (f32[8,2,8,128]{3,2,1,0:T(8,128)S(1)}, f32[8,2,8,128]{3,2,1,0:T(8,128)S(1)}, u32[]{:S(2)}, u32[]{:S(2)}) collective-permute-start(f32[8,2,8,128]{3,2,1,0:T(8,128)S(1)} %slice.343), channel_id=1, source_target_pairs={{0,2},{2,0},{4,6},{6,4},{8,10},{10,8},{12,14},{14,12},{16,18},{18,... | collective-permute-start | bytes 196616 | tf_op jit(solution)/shard_map/ppermute | solution.py:149
  163.4 14.8 %copy-start.4 = (bf16[8,768,128]{2,1,0:T(8,128)(2,1)S(1)}, bf16[8,768,128]{2,1,0:T(8,128)(2,1)}, u32[]{:S(2)}) copy-start(bf16[8,768,128]{2,1,0:T(8,128)(2,1)} %get-tuple-element.46) | copy-start | bytes 4718596
  165.7 16.2 %collective-permute-start.9 = (bf16[8,768,128]{2,1,0:T(8,128)(2,1)S(1)}, bf16[8,768,128]{2,1,0:T(8,128)(2,1)S(1)}, u32[]{:S(2)}, u32[]{:S(2)}) collective-permute-start(bf16[8,768,128]{2,1,0:T(8,128)(2,1)S(1)} %get-tuple-element.49), channel_id=1, source_target_pairs={{0,2},{2,0},{4,6},{6,4},{8,10},{10,8},{12,14},{14,12},{16,18},{18,... | collective-permute-start | bytes 4718600 | tf_op jit(solution)/shard_map/ppermute | solution.py:148
  165.9 5.0 %collective-permute-start.2 = (f32[4,2,8,128]{3,2,1,0:T(8,128)S(1)}, f32[4,2,8,128]{3,2,1,0:T(8,128)S(1)}, u32[]{:S(2)}, u32[]{:S(2)}) collective-permute-start(f32[4,2,8,128]{3,2,1,0:T(8,128)S(1)} %pad_maximum_fusion.3), channel_id=1, source_target_pairs={{0,4},{2,6},{4,0},{6,2},{8,12},{10,14},{12,8},{14,10},{16,20},{18,... | collective-permute-start | bytes 98312 | tf_op jit(solution)/shard_map/ppermute | solution.py:149
  169.0 4.0 %collective-permute-start.10 = (f32[4,2,8,128]{3,2,1,0:T(8,128)S(1)}, f32[4,2,8,128]{3,2,1,0:T(8,128)S(1)}, u32[]{:S(2)}, u32[]{:S(2)}) collective-permute-start(f32[4,2,8,128]{3,2,1,0:T(8,128)S(1)} %pad_maximum_fusion.2), channel_id=1, source_target_pairs={{0,4},{2,6},{4,0},{6,2},{8,12},{10,14},{12,8},{14,10},{16,20},{18,... | collective-permute-start | bytes 98312 | tf_op jit(solution)/shard_map/ppermute | solution.py:149
  170.9 3.8 %collective-permute-start.4 = (f32[2,2,8,128]{3,2,1,0:T(8,128)S(1)}, f32[2,2,8,128]{3,2,1,0:T(8,128)S(1)}, u32[]{:S(2)}, u32[]{:S(2)}) collective-permute-start(f32[2,2,8,128]{3,2,1,0:T(8,128)S(1)} %pad_maximum_fusion.5), channel_id=1, source_target_pairs={{0,8},{2,10},{4,12},{6,14},{8,0},{10,2},{12,4},{14,6},{16,24},{18,... | collective-permute-start | bytes 49160 | tf_op jit(solution)/shard_map/ppermute | solution.py:149
  173.1 10.2 %collective-permute-start.12 = (f32[2,2,8,128]{3,2,1,0:T(8,128)S(1)}, f32[2,2,8,128]{3,2,1,0:T(8,128)S(1)}, u32[]{:S(2)}, u32[]{:S(2)}) collective-permute-start(f32[2,2,8,128]{3,2,1,0:T(8,128)S(1)} %pad_maximum_fusion.4), channel_id=1, source_target_pairs={{0,8},{2,10},{4,12},{6,14},{8,0},{10,2},{12,4},{14,6},{16,24},{18,... | collective-permute-start | bytes 49160 | tf_op jit(solution)/shard_map/ppermute | solution.py:149
  174.8 8.6 %collective-permute-start.6 = (f32[1,2,8,128]{3,2,1,0:T(8,128)S(1)}, f32[1,2,8,128]{3,2,1,0:T(8,128)S(1)}, u32[]{:S(2)}, u32[]{:S(2)}) collective-permute-start(f32[1,2,8,128]{3,2,1,0:T(8,128)S(1)} %pad_maximum_fusion.7), channel_id=1, source_target_pairs={{0,16},{2,18},{4,20},{6,22},{8,24},{10,26},{12,28},{14,30},{16,0},... | collective-permute-start | bytes 24584 | tf_op jit(solution)/shard_map/ppermute | solution.py:149
  180.3 20.5 %collective-permute-start.3 = (bf16[4,768,128]{2,1,0:T(8,128)(2,1)S(1)}, bf16[4,768,128]{2,1,0:T(8,128)(2,1)S(1)}, u32[]{:S(2)}, u32[]{:S(2)}) collective-permute-start(bf16[4,768,128]{2,1,0:T(8,128)(2,1)S(1)} %bitcast.88), channel_id=1, source_target_pairs={{0,4},{2,6},{4,0},{6,2},{8,12},{10,14},{12,8},{14,10},{16,20},{18,... | collective-permute-start | bytes 2359304 | tf_op jit(solution)/shard_map/ppermute | solution.py:148
  182.7 31.9 %collective-permute-start.11 = (bf16[4,768,128]{2,1,0:T(8,128)(2,1)S(1)}, bf16[4,768,128]{2,1,0:T(8,128)(2,1)S(1)}, u32[]{:S(2)}, u32[]{:S(2)}) collective-permute-start(bf16[4,768,128]{2,1,0:T(8,128)(2,1)S(1)} %bitcast.89), channel_id=1, source_target_pairs={{0,4},{2,6},{4,0},{6,2},{8,12},{10,14},{12,8},{14,10},{16,20},{18,... | collective-permute-start | bytes 2359304 | tf_op jit(solution)/shard_map/ppermute | solution.py:148
  183.3 33.5 %collective-permute-start.14 = (f32[1,2,8,128]{3,2,1,0:T(8,128)S(1)}, f32[1,2,8,128]{3,2,1,0:T(8,128)S(1)}, u32[]{:S(2)}, u32[]{:S(2)}) collective-permute-start(f32[1,2,8,128]{3,2,1,0:T(8,128)S(1)} %pad_maximum_fusion.6), channel_id=1, source_target_pairs={{0,16},{2,18},{4,20},{6,22},{8,24},{10,26},{12,28},{14,30},{16,0},... | collective-permute-start | bytes 24584 | tf_op jit(solution)/shard_map/ppermute | solution.py:149
  201.2 15.5 %collective-permute-start.5 = (bf16[2,768,128]{2,1,0:T(8,128)(2,1)S(1)}, bf16[2,768,128]{2,1,0:T(8,128)(2,1)S(1)}, u32[]{:S(2)}, u32[]{:S(2)}) collective-permute-start(bf16[2,768,128]{2,1,0:T(8,128)(2,1)S(1)} %bitcast.94), channel_id=1, source_target_pairs={{0,8},{2,10},{4,12},{6,14},{8,0},{10,2},{12,4},{14,6},{16,24},{18,... | collective-permute-start | bytes 1179656 | tf_op jit(solution)/shard_map/ppermute | solution.py:148
  215.1 12.4 %collective-permute-start.13 = (bf16[2,768,128]{2,1,0:T(8,128)(2,1)S(1)}, bf16[2,768,128]{2,1,0:T(8,128)(2,1)S(1)}, u32[]{:S(2)}, u32[]{:S(2)}) collective-permute-start(bf16[2,768,128]{2,1,0:T(8,128)(2,1)S(1)} %bitcast.95), channel_id=1, source_target_pairs={{0,8},{2,10},{4,12},{6,14},{8,0},{10,2},{12,4},{14,6},{16,24},{18,... | collective-permute-start | bytes 1179656 | tf_op jit(solution)/shard_map/ppermute | solution.py:148
  216.9 10.8 %collective-permute-start.7 = (bf16[1,768,128]{2,1,0:T(8,128)(2,1)S(1)}, bf16[1,768,128]{2,1,0:T(8,128)(2,1)S(1)}, u32[]{:S(2)}, u32[]{:S(2)}) collective-permute-start(bf16[1,768,128]{2,1,0:T(8,128)(2,1)S(1)} %bitcast.98), channel_id=1, source_target_pairs={{0,16},{2,18},{4,20},{6,22},{8,24},{10,26},{12,28},{14,30},{16,0},... | collective-permute-start | bytes 589832 | tf_op jit(solution)/shard_map/ppermute | solution.py:148
  227.7 8.6 %collective-permute-start.15 = (bf16[1,768,128]{2,1,0:T(8,128)(2,1)S(1)}, bf16[1,768,128]{2,1,0:T(8,128)(2,1)S(1)}, u32[]{:S(2)}, u32[]{:S(2)}) collective-permute-start(bf16[1,768,128]{2,1,0:T(8,128)(2,1)S(1)} %bitcast.99), channel_id=1, source_target_pairs={{0,16},{2,18},{4,20},{6,22},{8,24},{10,26},{12,28},{14,30},{16,0},... | collective-permute-start | bytes 589832 | tf_op jit(solution)/shard_map/ppermute | solution.py:148
Sparse Core Ops, SparseCore 0:
  41.7 46.6 all-gather.2
  90.7 44.0 all-gather.4

commit v2 on v1

v2 whole, which is shorter than its diff:
```python
import functools
import jax
import jax.numpy as jnp
from jax import lax
from jax.experimental import pallas as pl
from jax.experimental.pallas import tpu as pltpu
from jax.sharding import PartitionSpec as P

EPSILON = 1e-05
FLOOR = -1e30
MASKED = -2e30
MSCALE = 1.1902380714238083
GROUP = 4


def rotate_rows(vectors, cosine, sine):
    half = vectors.shape[1] // 2
    front, back = vectors[:, :half], vectors[:, half:]
    return jnp.concatenate([front * cosine - back * sine, back * cosine + front * sine], axis=1)


def attend_kernel(
    owner_ref, bound_ref, place_ref, first_ref,
    near_ref, far_ref, k_ref, v_ref, nk_ref, nv_ref,
    keep_ref, send_ref, keep_stat_ref, send_stat_ref, acc, peak, total,
    *, requests, pairs, head_dim,
):
    rows = near_ref.shape[2]
    blocks, slots = k_ref.shape[0], k_ref.shape[1]
    width = 2 * pairs * rows
    acc[...] = jnp.zeros_like(acc)
    peak[...] = jnp.full_like(peak, FLOOR)
    total[...] = jnp.zeros_like(total)

    def step(request, keys, values, mask):
        for head in range(GROUP):
            span = slice(head * head_dim, (head + 1) * head_dim)
            queries = jnp.concatenate(
                [ref[request * pairs + c, span, :] for ref in (near_ref, far_ref) for c in range(pairs)],
                axis=1,
            )
            scores = jnp.dot(keys[:, span], queries, preferred_element_type=jnp.float32)
            scores = jnp.where(mask, scores, MASKED)
            old = peak[request, head : head + 1, :]
            new = jnp.maximum(old, jnp.max(scores, axis=0, keepdims=True))
            weight = jnp.exp(scores - new)
            fade = jnp.exp(old - new)
            peak[request, head : head + 1, :] = new
            total[request, head : head + 1, :] = total[request, head : head + 1, :] * fade + jnp.sum(
                weight, axis=0, keepdims=True
            )
            term = lax.dot_general(
                values[:, span], weight.astype(jnp.bfloat16), (((0,), (0,)), ((), ())),
                preferred_element_type=jnp.float32,
            )
            acc[request, span, :] = acc[request, span, :] * fade + term

    own_rows = nk_ref.shape[0]
    key_at = lax.broadcasted_iota(jnp.int32, (own_rows, width), 0) + first_ref[1]
    lane = lax.broadcasted_iota(jnp.int32, (own_rows, rows), 1)
    query_at = jnp.concatenate(
        [lane + (2 * c + first_ref[2 + side]) * rows for side in range(2) for c in range(pairs)], axis=1
    )
    step(first_ref[0], nk_ref[...], nv_ref[...], key_at <= query_at)

    slot_at = lax.broadcasted_iota(jnp.int32, (slots, width), 0)

    def one_block(block, carry):
        @pl.when(bound_ref[block] > 0)
        def _():
            step(owner_ref[block], k_ref[block], v_ref[block], slot_at < bound_ref[block])

        return carry

    lax.fori_loop(0, blocks, one_block, 0)

    for request in range(requests):
        for c in range(2 * pairs):
            out_ref, stat_ref = ((keep_ref, keep_stat_ref), (send_ref, send_stat_ref))[c // pairs]
            chunk = slice(c * rows, (c + 1) * rows)
            where_to = place_ref[request * pairs + c % pairs]
            out_ref[where_to] = acc[request, :, chunk].astype(jnp.bfloat16)
            stat_ref[where_to, 0] = jnp.concatenate(
                [peak[request, :, chunk], total[request, :, chunk]], axis=0
            )


def attend(scalars, near, far, keys, values, new_keys, new_values, part, requests, head_dim):
    half, feats, rows = near.shape
    blocks, slots = keys.shape[:2]
    span = GROUP * head_dim
    groups = feats // span
    pairs = half // requests
    own_rows = new_keys.shape[0]
    width = 2 * pairs * rows
    work = (blocks + 1) * slots * width * feats
    base = part * groups
    return pl.pallas_call(
        functools.partial(attend_kernel, requests=requests, pairs=pairs, head_dim=head_dim),
        grid_spec=pltpu.PrefetchScalarGridSpec(
            num_scalar_prefetch=4,
            grid=(groups,),
            in_specs=[
                pl.BlockSpec((half, span, rows), lambda g, *_: (0, g, 0)),
                pl.BlockSpec((half, span, rows), lambda g, *_: (0, g, 0)),
                pl.BlockSpec((blocks, slots, span), lambda g, *_: (0, 0, base + g)),
                pl.BlockSpec((blocks, slots, span), lambda g, *_: (0, 0, base + g)),
                pl.BlockSpec((own_rows, span), lambda g, *_: (0, base + g)),
                pl.BlockSpec((own_rows, span), lambda g, *_: (0, base + g)),
            ],
            out_specs=[
                pl.BlockSpec((half, span, rows), lambda g, *_: (0, g, 0)),
                pl.BlockSpec((half, span, rows), lambda g, *_: (0, g, 0)),
                pl.BlockSpec((half, 1, 2 * GROUP, rows), lambda g, *_: (0, g, 0, 0)),
                pl.BlockSpec((half, 1, 2 * GROUP, rows), lambda g, *_: (0, g, 0, 0)),
            ],
            scratch_shapes=[
                pltpu.VMEM((requests, span, width), jnp.float32),
                pltpu.VMEM((requests, GROUP, width), jnp.float32),
                pltpu.VMEM((requests, GROUP, width), jnp.float32),
            ],
        ),
        out_shape=[jax.ShapeDtypeStruct((half, feats, rows), jnp.bfloat16)] * 2
        + [jax.ShapeDtypeStruct((half, groups, 2 * GROUP, rows), jnp.float32)] * 2,
        compiler_params=pltpu.CompilerParams(vmem_limit_bytes=40 * 1024 * 1024),
        cost_estimate=pl.CostEstimate(
            flops=16 * work, bytes_accessed=8 * near.size + 4 * keys.size,
            transcendentals=work // head_dim,
        ),
    )(*scalars, near, far, keys, values, new_keys, new_values)


def merge(part_a, part_b, head_dim):
    out_a, stat_a = part_a
    out_b, stat_b = part_b
    count, groups, _, rows = stat_a.shape
    peak_a, peak_b = stat_a[:, :, :GROUP], stat_b[:, :, :GROUP]
    top = jnp.maximum(peak_a, peak_b)
    fade_a, fade_b = jnp.exp(peak_a - top), jnp.exp(peak_b - top)
    total = stat_a[:, :, GROUP:] * fade_a + stat_b[:, :, GROUP:] * fade_b
    shape = (count, groups, GROUP, head_dim, rows)
    out = (
        out_a.reshape(shape).astype(jnp.float32) * fade_a[:, :, :, None]
        + out_b.reshape(shape).astype(jnp.float32) * fade_b[:, :, :, None]
    )
    return out, top, total


def swap(array, bit, seq):
    return lax.ppermute(array, "seq", [(i, i ^ bit) for i in range(seq)])


def exchange(keep, send, bit, seq, head_dim):
    came = (swap(send[0], bit, seq), swap(send[1], bit, seq))
    half = keep[0].shape[0] // 2

    def side(part):
        merged, top, total = merge((keep[0][part], keep[1][part]), (came[0][part], came[1][part]), head_dim)
        shape = (half,) + keep[0].shape[1:]
        return merged.astype(jnp.bfloat16).reshape(shape), jnp.concatenate([top, total], axis=2)

    send_next = side(slice(half, 2 * half))
    return side(slice(0, half)), send_next


def finish(keep, send, bit, seq, head_dim):
    while 2 * bit < seq:
        keep, send = exchange(keep, send, bit, seq, head_dim)
        bit *= 2
    came = (swap(send[0], bit, seq), swap(send[1], bit, seq))
    merged, _, total = merge(keep, came, head_dim)
    return merged[0] / total[0][:, :, None]


def local(features, gain, w_qkv, rope_factors, cache_len, cache_kv, block_owner, block_base):
    rows = features.shape[0]
    seq = lax.axis_size("seq")
    me = lax.axis_index("seq")
    wide_x = lax.all_gather(features, "tensor", axis=1, tiled=True)
    wide_x, cache_keys = lax.optimization_barrier((wide_x, cache_kv[:, :, 0]))
    wide_x = wide_x.astype(jnp.float32)
    normed = (
        wide_x * lax.rsqrt(jnp.mean(wide_x * wide_x, axis=1, keepdims=True) + EPSILON) * gain
    ).astype(jnp.bfloat16)
    normed, cache_late = lax.optimization_barrier((normed, cache_kv))
    projected = jnp.einsum("td,dcf->cft", normed, w_qkv, preferred_element_type=jnp.float32)
    feats = projected.shape[1]
    head_dim = 2 * rope_factors.shape[0]
    heads = feats // head_dim
    requests = cache_len.shape[0]
    per_request = seq // requests
    request = me // per_request
    first_row = (me % per_request) * rows
    positions = cache_len[request] + first_row + jnp.arange(rows, dtype=jnp.int32)
    inv_freq = 1.0 / (
        rope_factors
        * jnp.power(10000.0, jnp.arange(rope_factors.shape[0], dtype=jnp.float32) * 2.0 / head_dim)
    )
    angles = inv_freq[None, :, None] * positions.astype(jnp.float32)[None, None, :]
    cosine, sine = jnp.cos(angles) * MSCALE, jnp.sin(angles) * MSCALE
    shaped = projected.reshape(3, heads, head_dim, rows)
    queries = (rotate_rows(shaped[0], cosine, sine) * head_dim ** (-0.5)).astype(jnp.bfloat16)
    new_keys = rotate_rows(shaped[1], cosine, sine).astype(jnp.bfloat16).reshape(feats, rows).T
    new_values = shaped[2].astype(jnp.bfloat16).reshape(feats, rows).T
    new_kv = jnp.stack([new_keys, new_values], axis=1)

    clamped = jnp.minimum(block_owner, requests - 1)
    bound = jnp.where(block_owner < requests, cache_len[clamped] - block_base, 0)
    place = jnp.zeros((seq // 2,), jnp.int32)
    flipped = jnp.arange(seq // 2, dtype=jnp.int32) ^ (me // 2)
    bit = 1
    while bit < seq // 2:
        place = place * 2 + (flipped // bit) % 2
        bit *= 2
    side = me % 2
    first = jnp.stack([request, first_row, side, 1 - side]).astype(jnp.int32)
    scalars = (clamped, bound, place, first)
    cache_values = cache_late[:, :, 1]
    queries = queries.reshape(feats, rows)

    groups = heads // GROUP
    parts = 2 if groups % 2 == 0 else 1
    wide = feats // parts
    same_side = [list(range(core, seq, 2)) for core in range(2)]
    near = [
        lax.all_gather(queries[i * wide : (i + 1) * wide], "seq", axis=0, axis_index_groups=same_side)
        for i in range(parts)
    ]
    far = [swap(part, 1, seq) for part in near]
    states = []
    for i in range(parts):
        here, there = near[i], far[i]
        if states:
            states[-1], here, there = lax.optimization_barrier((states[-1], here, there))
        keep, send, keep_stat, send_stat = attend(
            scalars, here, there, cache_keys, cache_values, new_keys, new_values, i, requests, head_dim
        )
        states.append(exchange((keep, keep_stat), (send, send_stat), 1, seq, head_dim))
    results = [finish(keep, send, 2, seq, head_dim).reshape(wide, rows) for keep, send in states]
    attended = jnp.concatenate(results, axis=0).astype(jnp.bfloat16).T
    return (attended, new_kv)


def solution(mesh):
    in_specs = (
        P("seq", "tensor"),
        P(),
        P(None, None, "tensor"),
        P(),
        P(),
        P("seq", None, None, "tensor"),
        P("seq"),
        P("seq"),
    )
    out_specs = (P("seq", "tensor"), P("seq", None, "tensor"))
    return jax.shard_map(local, mesh=mesh, in_specs=in_specs, out_specs=out_specs, check_vma=False)
```

time: 245 us -> 237 us (0.967)
  local copies, waits for them, and re-layouts: 57.3 us -> 35 us
  waiting for transfers between devices: 73.5 us -> 88.6 us
  Pallas kernels: 49 us -> 43.6 us
  starting transfers between devices: 18.1 us -> 23 us
    all_gather x2, waiting for transfers between devices: 19.8 us -> 52.2 us  [local(): lax.all_gather(queries[i * wide:(i + 1) * wide], 'seq', axis=0, axis_inde...]
    slice x14 -> x7, local copies, waits for them, and re-layouts: 31.1 us -> 0.24 us  [the longest x5 0.16 us: side(): came[0][part]]
    ppermute x16 -> x18, waiting for transfers between devices: 53.2 us -> 35.7 us  [swap(): return lax.ppermute(array, 'seq', [(i, i ^ bit) for i in range(seq)])]
    optimization_barrier x0 -> x1, local copies, waits for them, and re-layouts: none -> 9.42 us  [local(): normed, cache_late = lax.optimization_barrier((normed, cache_kv))]
    squeeze x1, local copies, waits for them, and re-layouts: 10.7 us -> 4.94 us  [local(): cache_values = cache_late[:, :, 1]]
    pallas_call x2, Pallas kernels: 49 us -> 43.6 us  [attend(): pl.pallas_call(functools.partial(attend_kernel, requests=requests, pairs=...]
    ppermute x16 -> x18, starting transfers between devices: 17.8 us -> 22.9 us  [swap(): return lax.ppermute(array, 'seq', [(i, i ^ bit) for i in range(seq)])]
    unnamed x16 -> x23, local copies, waits for them, and re-layouts: 7.63 us -> 12.6 us
  transfers between devices with their start and end apart: 18 -> 20, of which waited for: 9 -> 11; matrix products, arithmetic and copies ran while one was open for 20% -> 9% of each run, Pallas kernels for 20% -> 18%
where the time goes in v2:
time: 237 us; the launch traced here: 236 us
  waiting for transfers between devices  88.6 us (37%)
  Pallas kernels  43.6 us (18%)
  local copies, waits for them, and re-layouts  35 us (15%)
  starting transfers between devices  23 us (10%)
  between operations  15.1 us (6%)
  blocking collectives  12.8 us (5%)
  matrix products  11.1 us (5%)
  other arithmetic  7.14 us (3%)
    all_gather x2, waiting for transfers between devices, local(): lax.all_gather(queries[i * wide:(i + 1) * wide], 'seq', axis=0, axis_inde...  52.2 us
    pallas_call x2, Pallas kernels, attend(): pl.pallas_call(functools.partial(attend_kernel, requests=requests, pairs=...  43.6 us
    ppermute x18, waiting for transfers between devices, swap(): return lax.ppermute(array, 'seq', [(i, i ^ bit) for i in range(seq)])  35.7 us
    ppermute x18, starting transfers between devices, swap(): return lax.ppermute(array, 'seq', [(i, i ^ bit) for i in range(seq)])  22.9 us
    all_gather x1, blocking collectives, local(): wide_x = lax.all_gather(features, 'tensor', axis=1, tiled=True)  12.8 us
    unnamed x23, local copies, waits for them, and re-layouts  12.6 us
    dot_general x1, matrix products, local(): jnp.einsum('td,dcf->cft', normed, w_qkv, preferred_element_type=jnp.float32)  11.1 us
    optimization_barrier x1, local copies, waits for them, and re-layouts, local(): normed, cache_late = lax.optimization_barrier((normed, cache_kv))  9.42 us
  transfers between devices with their start and end apart: 20, of which 11 were waited for; matrix products, arithmetic and copies ran while one was open for 9% of the time, Pallas kernels for 18%

profile of v2, /device:TPU:0, one launch (start us, length us, event | category | flops | bytes accessed | tf_op | source)
XLA Modules:
  0.0 236.5 jit_solution(6357268635180978998)
XLA Ops:
  7.2 1.2 dynamic_slice.3
  9.1 0.7 multiply_divide_fusion
  9.8 7.4 %copy.35 = bf16[12,128,1,1536]{3,1,0,2:T(8,128)(2,1)} copy(bf16[12,128,1,1536]{3,2,1,0:T(2,128)(2,1)} %bitcast.153) | data formatting | bytes 9437184
  17.2 12.8 %all_gather.15 = bf16[128,3072]{1,0:T(8,128)(2,1)S(1)} all-gather(bf16[128,1536]{1,0:T(8,128)(2,1)S(1)} %copy-done.4), channel_id=1, replica_groups=mesh['seq'=16,'tensor'=2] {'tensor'}, dimensions={1}, use_global_device_ids=true | all-gather | bytes 1179648 | tf_op jit(solution)/shard_map/all_gather | solution.py:179
  30.1 0.2 fusion
  30.3 0.3 fusion.2
  30.6 11.1 %convolution_bitcast_fusion = f32[3,1536,128]{1,2,0:T(8,128)S(1)} fusion(bf16[3072,3,1536]{2,0,1:T(8,128)(2,1)} %param.10, bf16[128,3072]{1,0:T(8,128)(2,1)S(1)} %fusion.2), kind=kOutput, calls=%fused_computation.3 | convolution fusion | flops 3623878656 | bytes 31457280 | tf_op jit(solution)/shard_map/td,dcf->cft/dot_general | solution.py:186
  41.7 1.3 fusion.77
  43.0 1.4 copy.29
  44.4 2.3 copy.27
  46.7 0.2 fusion.35
  46.8 1.3 subtract_convert_fusion
  48.2 0.1 fusion.11
  48.3 0.8 fusion.80
  49.1 0.7 all-gather.5.cloned.1.call-update
  49.8 0.2 copy.30
  50.1 9.4 %copy.28 = bf16[12,128,2,1536]{3,1,0,2:T(8,128)(2,1)} copy(bf16[12,128,2,1536]{3,2,1,0:T(2,128)(2,1)} %param.13) | data formatting | bytes 18874368 | tf_op jit(solution)/shard_map/optimization_barrier | solution.py:185
  59.5 0.7 gather_fusion
  60.2 34.7 %all-gather.3.cloned.1.call-done.near_ref = bf16[8,768,128]{2,1,0:T(8,128)(2,1)} async-done(((bf16[1,768,128]{2,1,0:T(8,128)(2,1)}), bf16[8,768,128]{2,1,0:T(8,128)(2,1)}) %all-gather.3.cloned.1.call-update) | async-done | bytes 1572880 | tf_op jit(solution)/shard_map/all_gather | solution.py:226
  94.9 0.1 pad_add_fusion.first_ref
  95.1 4.9 %slice_bitcast_fusion.v_ref = bf16[12,128,1536]{2,1,0:T(8,128)(2,1)} fusion(bf16[12,128,2,1536]{3,1,0,2:T(8,128)(2,1)} %copy.28), kind=kLoop, calls=%fused_computation.1 | loop fusion | bytes 9437184 | tf_op jit(solution)/shard_map/squeeze | solution.py:218
  100.0 0.2 copy-done.2
  100.2 22.3 %shard_map.95 = (bf16[8,768,128]{2,1,0:T(8,128)(2,1)S(1)}, bf16[8,768,128]{2,1,0:T(8,128)(2,1)}, f32[8,2,8,128]{3,2,1,0:T(8,128)S(1)}, f32[8,2,8,128]{3,2,1,0:T(8,128)S(1)}) custom-call(s32[12]{0:T(128)S(1)} %get-tuple-element.143.owner_ref, s32[12]{0:T(128)S(1)} %get-tuple-element.142.bound_ref, s32[8]{0:T(128)S(1)} %fusion.68.place_ref, ...), custom_call_target="tpu_custom_call" | custom-call | flops 10468982784 | bytes 15728640 | tf_op jit(solution)/shard_map/pallas_call | solution.py:98
  122.5 0.5 collective-permute-start.2
  123.0 17.5 %all-gather.5.cloned.1.call-done.near_ref = bf16[8,768,128]{2,1,0:T(8,128)(2,1)} async-done(((bf16[1,768,128]{2,1,0:T(8,128)(2,1)}), bf16[8,768,128]{2,1,0:T(8,128)(2,1)}) %all-gather.5.cloned.1.call-update) | async-done | bytes 1572880 | tf_op jit(solution)/shard_map/all_gather | solution.py:226
  140.5 0.5 collective-permute-start.1
  141.0 2.6 %collective-permute-done.1 = f32[8,2,8,128]{3,2,1,0:T(8,128)S(1)} collective-permute-done((f32[8,2,8,128]{3,2,1,0:T(8,128)S(1)}, f32[8,2,8,128]{3,2,1,0:T(8,128)S(1)}, u32[]{:S(2)}, u32[]{:S(2)}) %collective-permute-start.1) | collective-permute-done | bytes 65568 | tf_op jit(solution)/shard_map/ppermute | solution.py:150
  143.7 2.0 fusion.8
  145.7 0.6 collective-permute-start.4
  146.4 0.1 pad_maximum_fusion
  146.4 1.7 copy.32
  148.1 1.5 collective-permute-start.5
  149.6 0.1 collective-permute-done.4
  149.8 2.0 collective-permute-start.6
  151.7 2.3 copy-done
  154.0 21.4 %shard_map.96 = (bf16[8,768,128]{2,1,0:T(8,128)(2,1)S(1)}, bf16[8,768,128]{2,1,0:T(8,128)(2,1)S(1)}, f32[8,2,8,128]{3,2,1,0:T(8,128)S(1)}, f32[8,2,8,128]{3,2,1,0:T(8,128)S(1)}) custom-call(s32[12]{0:T(128)S(1)} %get-tuple-element.143.owner_ref, s32[12]{0:T(128)S(1)} %get-tuple-element.142.bound_ref, s32[8]{0:T(128)S(1)} %fusion.68.place_ref, ...), custom_call_target="tpu_custom_call" | custom-call | flops 10468982784 | bytes 15728640 | tf_op jit(solution)/shard_map/pallas_call | solution.py:98
  175.5 0.5 collective-permute-start.11
  176.1 0.7 collective-permute-done.10
  176.8 2.9 %collective-permute-start.12 = (f32[4,2,8,128]{3,2,1,0:T(8,128)S(1)}, f32[4,2,8,128]{3,2,1,0:T(8,128)S(1)}, u32[]{:S(2)}, u32[]{:S(2)}) collective-permute-start(f32[4,2,8,128]{3,2,1,0:T(8,128)S(1)} %pad_maximum_fusion.4), channel_id=1, source_target_pairs={{0,4},{2,6},{4,0},{6,2},{8,12},{10,14},{12,8},{14,10},{16,20},{18,... | collective-permute-start | bytes 98312 | tf_op jit(solution)/shard_map/ppermute | solution.py:150
  179.7 0.8 collective-permute-start.8
  180.5 1.1 collective-permute-done.12
  181.7 3.9 %collective-permute-start.14 = (f32[2,2,8,128]{3,2,1,0:T(8,128)S(1)}, f32[2,2,8,128]{3,2,1,0:T(8,128)S(1)}, u32[]{:S(2)}, u32[]{:S(2)}) collective-permute-start(f32[2,2,8,128]{3,2,1,0:T(8,128)S(1)} %pad_maximum_fusion.6), channel_id=1, source_target_pairs={{0,8},{2,10},{4,12},{6,14},{8,0},{10,2},{12,4},{14,6},{16,24},{18,... | collective-permute-start | bytes 49160 | tf_op jit(solution)/shard_map/ppermute | solution.py:150
  185.5 1.7 collective-permute-done.14
  187.3 0.5 collective-permute-start.16
  187.8 0.3 fusion.6
  188.1 1.4 collective-permute-start.13
  189.5 2.5 %collective-permute-done.16 = f32[1,2,8,128]{3,2,1,0:T(8,128)S(1)} collective-permute-done((f32[1,2,8,128]{3,2,1,0:T(8,128)S(1)}, f32[1,2,8,128]{3,2,1,0:T(8,128)S(1)}, u32[]{:S(2)}, u32[]{:S(2)}) %collective-permute-start.16) | collective-permute-done | bytes 8224 | tf_op jit(solution)/shard_map/ppermute | solution.py:150
  192.1 0.2 fusion.19
  192.2 2.1 collective-permute-start.7
  194.4 0.2 fusion.15
  194.6 0.4 fusion.4
  195.0 10.4 %collective-permute-done.13 = bf16[4,768,128]{2,1,0:T(8,128)(2,1)S(1)} collective-permute-done((bf16[4,768,128]{2,1,0:T(8,128)(2,1)S(1)}, bf16[4,768,128]{2,1,0:T(8,128)(2,1)S(1)}, u32[]{:S(2)}, u32[]{:S(2)}) %collective-permute-start.13) | collective-permute-done | bytes 786464 | tf_op jit(solution)/shard_map/ppermute | solution.py:150
  205.4 0.2 fusion.13
  205.6 0.1 fusion.17
  205.8 2.0 collective-permute-start.15
  207.8 0.1 fusion.28
  207.9 2.5 %collective-permute-start.9 = (bf16[1,768,128]{2,1,0:T(8,128)(2,1)S(1)}, bf16[1,768,128]{2,1,0:T(8,128)(2,1)S(1)}, u32[]{:S(2)}, u32[]{:S(2)}) collective-permute-start(bf16[1,768,128]{2,1,0:T(8,128)(2,1)S(1)} %bitcast.169), channel_id=1, source_target_pairs={{0,16},{2,18},{4,20},{6,22},{8,24},{10,26},{12,28},{14,30},{16,0},... | collective-permute-start | bytes 589832 | tf_op jit(solution)/shard_map/ppermute | solution.py:150
  210.4 8.1 %collective-permute-done.15 = bf16[2,768,128]{2,1,0:T(8,128)(2,1)S(1)} collective-permute-done((bf16[2,768,128]{2,1,0:T(8,128)(2,1)S(1)}, bf16[2,768,128]{2,1,0:T(8,128)(2,1)S(1)}, u32[]{:S(2)}, u32[]{:S(2)}) %collective-permute-start.15) | collective-permute-done | bytes 393248 | tf_op jit(solution)/shard_map/ppermute | solution.py:150
  218.5 0.1 fusion.23
  218.6 1.2 collective-permute-start.17
  219.8 0.1 fusion.26
  220.0 8.5 %collective-permute-done.17 = bf16[1,768,128]{2,1,0:T(8,128)(2,1)S(1)} collective-permute-done((bf16[1,768,128]{2,1,0:T(8,128)(2,1)S(1)}, bf16[1,768,128]{2,1,0:T(8,128)(2,1)S(1)}, u32[]{:S(2)}, u32[]{:S(2)}) %collective-permute-start.17) | collective-permute-done | bytes 196640 | tf_op jit(solution)/shard_map/ppermute | solution.py:150
  228.5 0.1 fusion.21
  228.7 0.9 copy.31
  (68 shorter events, 1.0 us)
Async XLA Ops:
  7.2 87.7 %all-gather.3.cloned.1.call-start = ((), (), s32[]{:S(2)}) async-start(), calls=%async_computation | async-start | bytes 1769472 | tf_op jit(solution)/shard_map/all_gather | solution.py:226
  9.8 7.4 %copy-start.4 = (bf16[128,1536]{1,0:T(8,128)(2,1)S(1)}, bf16[128,1536]{1,0:T(8,128)(2,1)}, u32[]{:S(2)}) copy-start(bf16[128,1536]{1,0:T(8,128)(2,1)} %param.8) | copy-start | bytes 1179652
  17.2 13.1 %copy-start.5 = (f32[3072]{0:T(1024)S(1)}, f32[3072]{0:T(1024)}, u32[]{:S(2)}) copy-start(f32[3072]{0:T(1024)} %param.9) | copy-start | bytes 36868
  49.1 91.5 %all-gather.5.cloned.1.call-start = ((), (), s32[]{:S(2)}) async-start(), calls=%async_computation.1 | async-start | bytes 1769472 | tf_op jit(solution)/shard_map/all_gather | solution.py:226
  50.0 9.5 %copy-start.6 = (s32[12]{0:T(128)S(1)}, s32[12]{0:T(128)}, u32[]{:S(2)}) copy-start(s32[12]{0:T(128)} %param.14) | copy-start | bytes 148
  50.1 9.5 %copy-start.3 = (s32[4]{0:T(128)S(1)}, s32[4]{0:T(128)}, u32[]{:S(2)}) copy-start(s32[4]{0:T(128)} %param.12) | copy-start | bytes 52
  50.1 44.9 %copy-start.7 = (s32[12]{0:T(128)S(1)}, s32[12]{0:T(128)}, u32[]{:S(2)}) copy-start(s32[12]{0:T(128)} %param.15) | copy-start | bytes 148
  94.9 5.1 %collective-permute-start = (bf16[8,768,128]{2,1,0:T(8,128)(2,1)}, bf16[8,768,128]{2,1,0:T(8,128)(2,1)S(1)}, u32[]{:S(2)}, u32[]{:S(2)}) collective-permute-start(bf16[8,768,128]{2,1,0:T(8,128)(2,1)} %all-gather.3.cloned.1.call-done.near_ref), channel_id=1, source_target_pairs={{0,2},{2,0},{4,6},{6,4},{8,10},{10,8},{12,14},{14,12},{16,18},{18,... | collective-permute-start | bytes 4718600 | tf_op jit(solution)/shard_map/ppermute | solution.py:150
  95.0 5.0 %slice-start = ((s8[4718592]{0:T(1024)(128)(4,1)}), s8[4194304]{0:T(1024)(128)(4,1)S(1)}, s32[]{:S(2)}) async-start(s8[4718592]{0:T(1024)(128)(4,1)} %bitcast.146), calls=%async_computation.2 | async-start | bytes 8388608
  95.1 5.0 %slice-start.1 = ((s8[4718592]{0:T(1024)(128)(4,1)}), s8[524288]{0:T(1024)(128)(4,1)S(1)}, s32[]{:S(2)}) async-start(s8[4718592]{0:T(1024)(128)(4,1)} %bitcast.146), calls=%async_computation.3 | async-start | bytes 1048576
  95.1 5.1 %copy-start.2 = (bf16[8,768,128]{2,1,0:T(8,128)(2,1)S(1)}, bf16[8,768,128]{2,1,0:T(8,128)(2,1)}, u32[]{:S(2)}) copy-start(bf16[8,768,128]{2,1,0:T(8,128)(2,1)} %all-gather.3.cloned.1.call-done.near_ref) | copy-start | bytes 4718596
  122.5 21.2 %collective-permute-start.2 = (bf16[8,768,128]{2,1,0:T(8,128)(2,1)}, bf16[8,768,128]{2,1,0:T(8,128)(2,1)}, u32[]{:S(2)}, u32[]{:S(2)}) collective-permute-start(bf16[8,768,128]{2,1,0:T(8,128)(2,1)} %get-tuple-element.27), channel_id=1, source_target_pairs={{0,2},{2,0},{4,6},{6,4},{8,10},{10,8},{12,14},{14,12},{16,18},{18,... | collective-permute-start | bytes 4718600 | tf_op jit(solution)/shard_map/ppermute | solution.py:150
  140.5 5.2 %collective-permute-start.3 = (bf16[8,768,128]{2,1,0:T(8,128)(2,1)}, bf16[8,768,128]{2,1,0:T(8,128)(2,1)S(1)}, u32[]{:S(2)}, u32[]{:S(2)}) collective-permute-start(bf16[8,768,128]{2,1,0:T(8,128)(2,1)} %all-gather.5.cloned.1.call-done.near_ref), channel_id=1, source_target_pairs={{0,2},{2,0},{4,6},{6,4},{8,10},{10,8},{12,14},{14,12},{16,18},{18,... | collective-permute-start | bytes 4718600 | tf_op jit(solution)/shard_map/ppermute | solution.py:150
  140.5 3.1 %collective-permute-start.1 = (f32[8,2,8,128]{3,2,1,0:T(8,128)S(1)}, f32[8,2,8,128]{3,2,1,0:T(8,128)S(1)}, u32[]{:S(2)}, u32[]{:S(2)}) collective-permute-start(f32[8,2,8,128]{3,2,1,0:T(8,128)S(1)} %get-tuple-element.26), channel_id=1, source_target_pairs={{0,2},{2,0},{4,6},{6,4},{8,10},{10,8},{12,14},{14,12},{16,18},{18,... | collective-permute-start | bytes 196616 | tf_op jit(solution)/shard_map/ppermute | solution.py:150
  145.7 4.0 %collective-permute-start.4 = (f32[4,2,8,128]{3,2,1,0:T(8,128)S(1)}, f32[4,2,8,128]{3,2,1,0:T(8,128)S(1)}, u32[]{:S(2)}, u32[]{:S(2)}) collective-permute-start(f32[4,2,8,128]{3,2,1,0:T(8,128)S(1)} %get-tuple-element.30), channel_id=1, source_target_pairs={{0,4},{2,6},{4,0},{6,2},{8,12},{10,14},{12,8},{14,10},{16,20},{18,... | collective-permute-start | bytes 98312 | tf_op jit(solution)/shard_map/ppermute | solution.py:150
  146.4 5.4 %copy-start.1 = (bf16[8,768,128]{2,1,0:T(8,128)(2,1)S(1)}, bf16[8,768,128]{2,1,0:T(8,128)(2,1)}, u32[]{:S(2)}) copy-start(bf16[8,768,128]{2,1,0:T(8,128)(2,1)} %all-gather.5.cloned.1.call-done.near_ref) | copy-start | bytes 4718596
  148.1 43.9 %collective-permute-start.5 = (bf16[4,768,128]{2,1,0:T(8,128)(2,1)S(1)}, bf16[4,768,128]{2,1,0:T(8,128)(2,1)S(1)}, u32[]{:S(2)}, u32[]{:S(2)}) collective-permute-start(bf16[4,768,128]{2,1,0:T(8,128)(2,1)S(1)} %get-tuple-element.31), channel_id=1, source_target_pairs={{0,4},{2,6},{4,0},{6,2},{8,12},{10,14},{12,8},{14,10},{16,20},{18,... | collective-permute-start | bytes 2359304 | tf_op jit(solution)/shard_map/ppermute | solution.py:150
  149.8 26.3 %collective-permute-start.6 = (f32[2,2,8,128]{3,2,1,0:T(8,128)S(1)}, f32[2,2,8,128]{3,2,1,0:T(8,128)S(1)}, u32[]{:S(2)}, u32[]{:S(2)}) collective-permute-start(f32[2,2,8,128]{3,2,1,0:T(8,128)S(1)} %pad_maximum_fusion.5), channel_id=1, source_target_pairs={{0,8},{2,10},{4,12},{6,14},{8,0},{10,2},{12,4},{14,6},{16,24},{18,... | collective-permute-start | bytes 49160 | tf_op jit(solution)/shard_map/ppermute | solution.py:150
  151.7 2.3 copy-start
  175.4 1.3 collective-permute-start.10
  175.5 12.3 %collective-permute-start.11 = (bf16[8,768,128]{2,1,0:T(8,128)(2,1)S(1)}, bf16[8,768,128]{2,1,0:T(8,128)(2,1)S(1)}, u32[]{:S(2)}, u32[]{:S(2)}) collective-permute-start(bf16[8,768,128]{2,1,0:T(8,128)(2,1)S(1)} %get-tuple-element.37), channel_id=1, source_target_pairs={{0,2},{2,0},{4,6},{6,4},{8,10},{10,8},{12,14},{14,12},{16,18},{18,... | collective-permute-start | bytes 4718600 | tf_op jit(solution)/shard_map/ppermute | solution.py:150
  176.8 4.8 %collective-permute-start.12 = (f32[4,2,8,128]{3,2,1,0:T(8,128)S(1)}, f32[4,2,8,128]{3,2,1,0:T(8,128)S(1)}, u32[]{:S(2)}, u32[]{:S(2)}) collective-permute-start(f32[4,2,8,128]{3,2,1,0:T(8,128)S(1)} %pad_maximum_fusion.4), channel_id=1, source_target_pairs={{0,4},{2,6},{4,0},{6,2},{8,12},{10,14},{12,8},{14,10},{16,20},{18,... | collective-permute-start | bytes 98312 | tf_op jit(solution)/shard_map/ppermute | solution.py:150
  179.7 5.8 %collective-permute-start.8 = (f32[1,2,8,128]{3,2,1,0:T(8,128)S(1)}, f32[1,2,8,128]{3,2,1,0:T(8,128)S(1)}, u32[]{:S(2)}, u32[]{:S(2)}) collective-permute-start(f32[1,2,8,128]{3,2,1,0:T(8,128)S(1)} %pad_maximum_fusion.7), channel_id=1, source_target_pairs={{0,16},{2,18},{4,20},{6,22},{8,24},{10,26},{12,28},{14,30},{16,0},... | collective-permute-start | bytes 24584 | tf_op jit(solution)/shard_map/ppermute | solution.py:150
  181.7 5.6 %collective-permute-start.14 = (f32[2,2,8,128]{3,2,1,0:T(8,128)S(1)}, f32[2,2,8,128]{3,2,1,0:T(8,128)S(1)}, u32[]{:S(2)}, u32[]{:S(2)}) collective-permute-start(f32[2,2,8,128]{3,2,1,0:T(8,128)S(1)} %pad_maximum_fusion.6), channel_id=1, source_target_pairs={{0,8},{2,10},{4,12},{6,14},{8,0},{10,2},{12,4},{14,6},{16,24},{18,... | collective-permute-start | bytes 49160 | tf_op jit(solution)/shard_map/ppermute | solution.py:150
  187.3 4.7 %collective-permute-start.16 = (f32[1,2,8,128]{3,2,1,0:T(8,128)S(1)}, f32[1,2,8,128]{3,2,1,0:T(8,128)S(1)}, u32[]{:S(2)}, u32[]{:S(2)}) collective-permute-start(f32[1,2,8,128]{3,2,1,0:T(8,128)S(1)} %pad_maximum_fusion.8), channel_id=1, source_target_pairs={{0,16},{2,18},{4,20},{6,22},{8,24},{10,26},{12,28},{14,30},{16,0},... | collective-permute-start | bytes 24584 | tf_op jit(solution)/shard_map/ppermute | solution.py:150
  188.1 17.3 %collective-permute-start.13 = (bf16[4,768,128]{2,1,0:T(8,128)(2,1)S(1)}, bf16[4,768,128]{2,1,0:T(8,128)(2,1)S(1)}, u32[]{:S(2)}, u32[]{:S(2)}) collective-permute-start(bf16[4,768,128]{2,1,0:T(8,128)(2,1)S(1)} %fusion.6), channel_id=1, source_target_pairs={{0,4},{2,6},{4,0},{6,2},{8,12},{10,14},{12,8},{14,10},{16,20},{18,... | collective-permute-start | bytes 2359304 | tf_op jit(solution)/shard_map/ppermute | solution.py:150
  192.2 15.6 %collective-permute-start.7 = (bf16[2,768,128]{2,1,0:T(8,128)(2,1)S(1)}, bf16[2,768,128]{2,1,0:T(8,128)(2,1)S(1)}, u32[]{:S(2)}, u32[]{:S(2)}) collective-permute-start(bf16[2,768,128]{2,1,0:T(8,128)(2,1)S(1)} %fusion.19), channel_id=1, source_target_pairs={{0,8},{2,10},{4,12},{6,14},{8,0},{10,2},{12,4},{14,6},{16,24},{18,... | collective-permute-start | bytes 1179656 | tf_op jit(solution)/shard_map/ppermute | solution.py:150
  205.8 12.7 %collective-permute-start.15 = (bf16[2,768,128]{2,1,0:T(8,128)(2,1)S(1)}, bf16[2,768,128]{2,1,0:T(8,128)(2,1)S(1)}, u32[]{:S(2)}, u32[]{:S(2)}) collective-permute-start(bf16[2,768,128]{2,1,0:T(8,128)(2,1)S(1)} %fusion.17), channel_id=1, source_target_pairs={{0,8},{2,10},{4,12},{6,14},{8,0},{10,2},{12,4},{14,6},{16,24},{18,... | collective-permute-start | bytes 1179656 | tf_op jit(solution)/shard_map/ppermute | solution.py:150
  207.9 11.9 %collective-permute-start.9 = (bf16[1,768,128]{2,1,0:T(8,128)(2,1)S(1)}, bf16[1,768,128]{2,1,0:T(8,128)(2,1)S(1)}, u32[]{:S(2)}, u32[]{:S(2)}) collective-permute-start(bf16[1,768,128]{2,1,0:T(8,128)(2,1)S(1)} %bitcast.169), channel_id=1, source_target_pairs={{0,16},{2,18},{4,20},{6,22},{8,24},{10,26},{12,28},{14,30},{16,0},... | collective-permute-start | bytes 589832 | tf_op jit(solution)/shard_map/ppermute | solution.py:150
  218.6 9.9 %collective-permute-start.17 = (bf16[1,768,128]{2,1,0:T(8,128)(2,1)S(1)}, bf16[1,768,128]{2,1,0:T(8,128)(2,1)S(1)}, u32[]{:S(2)}, u32[]{:S(2)}) collective-permute-start(bf16[1,768,128]{2,1,0:T(8,128)(2,1)S(1)} %bitcast.168), channel_id=1, source_target_pairs={{0,16},{2,18},{4,20},{6,22},{8,24},{10,26},{12,28},{14,30},{16,0},... | collective-permute-start | bytes 589832 | tf_op jit(solution)/shard_map/ppermute | solution.py:150
Sparse Core Ops, SparseCore 0:
  49.2 45.6 all-gather.2
  97.6 42.8 all-gather.4

commit v3 on v2

--- a/solution.py
+++ b/solution.py
@@ -21,11 +21,11 @@
 
 def attend_kernel(
     owner_ref, bound_ref, place_ref, first_ref,
-    near_ref, far_ref, k_ref, v_ref, nk_ref, nv_ref,
+    q_ref, k_ref, v_ref, nk_ref, nv_ref,
     keep_ref, send_ref, keep_stat_ref, send_stat_ref, acc, peak, total,
     *, requests, pairs, head_dim,
 ):
-    rows = near_ref.shape[2]
+    rows = q_ref.shape[3]
     blocks, slots = k_ref.shape[0], k_ref.shape[1]
     width = 2 * pairs * rows
     acc[...] = jnp.zeros_like(acc)
@@ -36,7 +36,11 @@
         for head in range(GROUP):
             span = slice(head * head_dim, (head + 1) * head_dim)
             queries = jnp.concatenate(
-                [ref[request * pairs + c, span, :] for ref in (near_ref, far_ref) for c in range(pairs)],
+                [
+                    q_ref[request * pairs + c, first_ref[2 + side], span, :]
+                    for side in range(2)
+                    for c in range(pairs)
+                ],
                 axis=1,
             )
             scores = jnp.dot(keys[:, span], queries, preferred_element_type=jnp.float32)
@@ -85,8 +89,9 @@
             )
 
 
-def attend(scalars, near, far, keys, values, new_keys, new_values, part, requests, head_dim):
-    half, feats, rows = near.shape
+def attend(scalars, queries, keys, values, new_keys, new_values, part, parts, requests, head_dim):
+    half, _, feats, rows = queries.shape
+    feats = feats // parts
     blocks, slots = keys.shape[:2]
     span = GROUP * head_dim
     groups = feats // span
@@ -101,8 +106,7 @@
             num_scalar_prefetch=4,
             grid=(groups,),
             in_specs=[
-                pl.BlockSpec((half, span, rows), lambda g, *_: (0, g, 0)),
-                pl.BlockSpec((half, span, rows), lambda g, *_: (0, g, 0)),
+                pl.BlockSpec((half, 2, span, rows), lambda g, *_: (0, 0, base + g, 0)),
                 pl.BlockSpec((blocks, slots, span), lambda g, *_: (0, 0, base + g)),
                 pl.BlockSpec((blocks, slots, span), lambda g, *_: (0, 0, base + g)),
                 pl.BlockSpec((own_rows, span), lambda g, *_: (0, base + g)),
@@ -124,10 +128,10 @@
         + [jax.ShapeDtypeStruct((half, groups, 2 * GROUP, rows), jnp.float32)] * 2,
         compiler_params=pltpu.CompilerParams(vmem_limit_bytes=40 * 1024 * 1024),
         cost_estimate=pl.CostEstimate(
-            flops=16 * work, bytes_accessed=8 * near.size + 4 * keys.size,
+            flops=16 * work, bytes_accessed=4 * queries.size + 4 * keys.size,
             transcendentals=work // head_dim,
         ),
-    )(*scalars, near, far, keys, values, new_keys, new_values)
+    )(*scalars, queries, keys, values, new_keys, new_values)
 
 
 def merge(part_a, part_b, head_dim):
@@ -221,19 +225,14 @@
     groups = heads // GROUP
     parts = 2 if groups % 2 == 0 else 1
     wide = feats // parts
-    same_side = [list(range(core, seq, 2)) for core in range(2)]
-    near = [
-        lax.all_gather(queries[i * wide : (i + 1) * wide], "seq", axis=0, axis_index_groups=same_side)
-        for i in range(parts)
-    ]
-    far = [swap(part, 1, seq) for part in near]
+    gathered = lax.all_gather(queries, "seq", axis=0).reshape(seq // 2, 2, feats, rows)
     states = []
     for i in range(parts):
-        here, there = near[i], far[i]
+        here = gathered
         if states:
-            states[-1], here, there = lax.optimization_barrier((states[-1], here, there))
+            states[-1], here = lax.optimization_barrier((states[-1], here))
         keep, send, keep_stat, send_stat = attend(
-            scalars, here, there, cache_keys, cache_values, new_keys, new_values, i, requests, head_dim
+            scalars, here, cache_keys, cache_values, new_keys, new_values, i, parts, requests, head_dim
         )
         states.append(exchange((keep, keep_stat), (send, send_stat), 1, seq, head_dim))
     results = [finish(keep, send, 2, seq, head_dim).reshape(wide, rows) for keep, send in states]

time: 237 us -> 238 us (level)
  starting transfers between devices: 23 us -> 7.69 us
  Pallas kernels: 43.6 us -> 51.8 us
  waiting for transfers between devices: 88.6 us -> 93.9 us
    ppermute x18 -> x16, starting transfers between devices: 22.9 us -> 7.65 us  [swap(): return lax.ppermute(array, 'seq', [(i, i ^ bit) for i in range(seq)])]
    ppermute x18 -> x16, waiting for transfers between devices: 35.7 us -> 45.8 us  [swap(): return lax.ppermute(array, 'seq', [(i, i ^ bit) for i in range(seq)])]
    pallas_call x2, Pallas kernels: 43.6 us -> 51.8 us  [attend(): pl.pallas_call(functools.partial(attend_kernel, requests=requests, pairs=...]
    all_gather x2 -> x1, waiting for transfers between devices: 52.2 us -> 48.1 us  [local(): lax.all_gather(queries, 'seq', axis=0).reshape(seq // 2, 2, feats, rows)]
    unnamed x23 -> x17, local copies, waits for them, and re-layouts: 12.6 us -> 14.6 us
  transfers between devices with their start and end apart: 20 -> 17, of which waited for: 11 -> 12; matrix products, arithmetic and copies ran while one was open for 9% -> 8% of each run, Pallas kernels for 18% -> 11%
where the time goes in v3:
time: 238 us; the launch traced here: 235 us
  waiting for transfers between devices  93.9 us (39%)
  Pallas kernels  51.8 us (22%)
  local copies, waits for them, and re-layouts  36.1 us (15%)
  between operations  15.2 us (6%)
  blocking collectives  12.8 us (5%)
  matrix products  11.1 us (5%)
  starting transfers between devices  7.69 us (3%)
  other arithmetic  6.53 us (3%)
    pallas_call x2, Pallas kernels, attend(): pl.pallas_call(functools.partial(attend_kernel, requests=requests, pairs=...  51.8 us
    all_gather x1, waiting for transfers between devices, local(): lax.all_gather(queries, 'seq', axis=0).reshape(seq // 2, 2, feats, rows)  48.1 us
    ppermute x16, waiting for transfers between devices, swap(): return lax.ppermute(array, 'seq', [(i, i ^ bit) for i in range(seq)])  45.8 us
    unnamed x17, local copies, waits for them, and re-layouts  14.6 us
    all_gather x1, blocking collectives, local(): wide_x = lax.all_gather(features, 'tensor', axis=1, tiled=True)  12.8 us
    dot_general x1, matrix products, local(): jnp.einsum('td,dcf->cft', normed, w_qkv, preferred_element_type=jnp.float32)  11.1 us
    optimization_barrier x1, local copies, waits for them, and re-layouts, local(): normed, cache_late = lax.optimization_barrier((normed, cache_kv))  9.4 us
    ppermute x16, starting transfers between devices, swap(): return lax.ppermute(array, 'seq', [(i, i ^ bit) for i in range(seq)])  7.65 us
  transfers between devices with their start and end apart: 17, of which 12 were waited for; matrix products, arithmetic and copies ran while one was open for 8% of the time, Pallas kernels for 11%

profile of v3, /device:TPU:0, one launch (start us, length us, event | category | flops | bytes accessed | tf_op | source)
XLA Modules:
  0.0 235.2 jit_solution(14236956793372465977)
XLA Ops:
  7.2 1.2 dynamic_slice.3
  9.1 0.7 multiply_divide_fusion
  9.8 7.3 %copy.34 = bf16[12,128,1,1536]{3,1,0,2:T(8,128)(2,1)} copy(bf16[12,128,1,1536]{3,2,1,0:T(2,128)(2,1)} %bitcast.151) | data formatting | bytes 9437184
  17.1 12.8 %all_gather.6 = bf16[128,3072]{1,0:T(8,128)(2,1)S(1)} all-gather(bf16[128,1536]{1,0:T(8,128)(2,1)S(1)} %copy-done.3), channel_id=1, replica_groups=mesh['seq'=16,'tensor'=2] {'tensor'}, dimensions={1}, use_global_device_ids=true | all-gather | bytes 1179648 | tf_op jit(solution)/shard_map/all_gather | solution.py:183
  29.9 0.2 fusion
  30.2 0.3 fusion.2
  30.5 11.1 %convolution_bitcast_fusion = f32[3,1536,128]{1,2,0:T(8,128)S(1)} fusion(bf16[3072,3,1536]{2,0,1:T(8,128)(2,1)} %param.10, bf16[128,3072]{1,0:T(8,128)(2,1)S(1)} %fusion.2), kind=kOutput, calls=%fused_computation.3 | convolution fusion | flops 3623878656 | bytes 31457280 | tf_op jit(solution)/shard_map/td,dcf->cft/dot_general | solution.py:190
  41.6 1.3 fusion.77
  42.8 1.4 copy.28
  44.2 2.3 copy.26
  46.5 0.2 fusion.35
  46.7 1.3 subtract_convert_fusion
  48.0 0.8 fusion.11
  48.9 0.2 copy.29
  49.2 9.4 %copy.27 = bf16[12,128,2,1536]{3,1,0,2:T(8,128)(2,1)} copy(bf16[12,128,2,1536]{3,2,1,0:T(2,128)(2,1)} %param.13) | data formatting | bytes 18874368 | tf_op jit(solution)/shard_map/optimization_barrier | solution.py:189
  58.6 0.7 gather_fusion
  59.3 0.1 pad_add_fusion.first_ref
  59.4 4.8 %slice_bitcast_fusion.v_ref = bf16[12,128,1536]{2,1,0:T(8,128)(2,1)} fusion(bf16[12,128,2,1536]{3,1,0,2:T(8,128)(2,1)} %copy.27), kind=kLoop, calls=%fused_computation.1 | loop fusion | bytes 9437184 | tf_op jit(solution)/shard_map/squeeze | solution.py:222
  64.2 48.1 %all-gather.2.cloned.1.call-done = bf16[16,1536,128]{2,1,0:T(8,128)(2,1)} async-done(((bf16[1,1536,128]{2,1,0:T(8,128)(2,1)}), bf16[16,1536,128]{2,1,0:T(8,128)(2,1)}) %all-gather.2.cloned.1.call-update) | async-done | bytes 6291472 | tf_op jit(solution)/shard_map/all_gather | solution.py:228
  112.4 2.3 copy-done
  114.7 2.3 copy-done.1
  117.1 25.8 %shard_map.95 = (bf16[8,768,128]{2,1,0:T(8,128)(2,1)S(1)}, bf16[8,768,128]{2,1,0:T(8,128)(2,1)S(1)}, f32[8,2,8,128]{3,2,1,0:T(8,128)S(1)}, f32[8,2,8,128]{3,2,1,0:T(8,128)S(1)}) custom-call(s32[12]{0:T(128)S(1)} %get-tuple-element.139.owner_ref, s32[12]{0:T(128)S(1)} %get-tuple-element.138.bound_ref, s32[8]{0:T(128)S(1)} %fusion.68.place_ref, ...), custom_call_target="tpu_custom_call" | custom-call | flops 10468982784 | bytes 22020096 | tf_op jit(solution)/shard_map/pallas_call | solution.py:103
  142.9 0.1 collective-permute-start.1
  143.0 0.5 collective-permute-start
  143.5 3.0 %collective-permute-done = f32[8,2,8,128]{3,2,1,0:T(8,128)S(1)} collective-permute-done((f32[8,2,8,128]{3,2,1,0:T(8,128)S(1)}, f32[8,2,8,128]{3,2,1,0:T(8,128)S(1)}, u32[]{:S(2)}, u32[]{:S(2)}) %collective-permute-start) | collective-permute-done | bytes 65568 | tf_op jit(solution)/shard_map/ppermute | solution.py:154
  146.5 0.6 fusion.8
  147.1 0.5 collective-permute-start.2
  147.7 0.1 pad_maximum_fusion
  147.7 1.7 copy.31
  149.4 1.6 collective-permute-start.3
  151.0 0.1 collective-permute-done.2
  151.2 0.1 collective-permute-start.4
  151.2 26.0 %shard_map.96 = (bf16[8,768,128]{2,1,0:T(8,128)(2,1)S(1)}, bf16[8,768,128]{2,1,0:T(8,128)(2,1)S(1)}, f32[8,2,8,128]{3,2,1,0:T(8,128)S(1)}, f32[8,2,8,128]{3,2,1,0:T(8,128)S(1)}) custom-call(s32[12]{0:T(128)S(1)} %get-tuple-element.139.owner_ref, s32[12]{0:T(128)S(1)} %get-tuple-element.138.bound_ref, s32[8]{0:T(128)S(1)} %fusion.68.place_ref, ...), custom_call_target="tpu_custom_call" | custom-call | flops 10468982784 | bytes 22020096 | tf_op jit(solution)/shard_map/pallas_call | solution.py:103
  177.3 0.1 collective-permute-start.8
  177.4 0.5 collective-permute-start.9
  178.0 0.7 collective-permute-done.8
  178.7 0.1 collective-permute-start.10
  178.8 0.3 collective-permute-start.6
  179.0 3.6 %collective-permute-done.10 = f32[4,2,8,128]{3,2,1,0:T(8,128)S(1)} collective-permute-done((f32[4,2,8,128]{3,2,1,0:T(8,128)S(1)}, f32[4,2,8,128]{3,2,1,0:T(8,128)S(1)}, u32[]{:S(2)}, u32[]{:S(2)}) %collective-permute-start.10) | collective-permute-done | bytes 32800 | tf_op jit(solution)/shard_map/ppermute | solution.py:154
  182.7 0.1 collective-permute-start.12
  182.8 0.6 collective-permute-done.6
  183.4 3.1 %collective-permute-done.12 = f32[2,2,8,128]{3,2,1,0:T(8,128)S(1)} collective-permute-done((f32[2,2,8,128]{3,2,1,0:T(8,128)S(1)}, f32[2,2,8,128]{3,2,1,0:T(8,128)S(1)}, u32[]{:S(2)}, u32[]{:S(2)}) %collective-permute-start.12) | collective-permute-done | bytes 16416 | tf_op jit(solution)/shard_map/ppermute | solution.py:154
  186.5 0.5 collective-permute-start.14
  187.1 0.3 fusion.6
  187.4 0.7 collective-permute-start.11
  188.1 3.2 %collective-permute-done.14 = f32[1,2,8,128]{3,2,1,0:T(8,128)S(1)} collective-permute-done((f32[1,2,8,128]{3,2,1,0:T(8,128)S(1)}, f32[1,2,8,128]{3,2,1,0:T(8,128)S(1)}, u32[]{:S(2)}, u32[]{:S(2)}) %collective-permute-start.14) | collective-permute-done | bytes 8224 | tf_op jit(solution)/shard_map/ppermute | solution.py:154
  191.3 0.2 fusion.19
  191.5 0.1 collective-permute-start.5
  191.6 0.2 fusion.15
  191.8 0.4 fusion.4
  192.2 12.6 %collective-permute-done.11 = bf16[4,768,128]{2,1,0:T(8,128)(2,1)S(1)} collective-permute-done((bf16[4,768,128]{2,1,0:T(8,128)(2,1)S(1)}, bf16[4,768,128]{2,1,0:T(8,128)(2,1)S(1)}, u32[]{:S(2)}, u32[]{:S(2)}) %collective-permute-start.11) | collective-permute-done | bytes 786464 | tf_op jit(solution)/shard_map/ppermute | solution.py:154
  204.8 0.2 fusion.13
  205.0 0.1 fusion.17
  205.2 1.8 collective-permute-start.13
  207.0 0.1 fusion.28
  207.1 0.8 collective-permute-start.7
  207.9 9.5 %collective-permute-done.13 = bf16[2,768,128]{2,1,0:T(8,128)(2,1)S(1)} collective-permute-done((bf16[2,768,128]{2,1,0:T(8,128)(2,1)S(1)}, bf16[2,768,128]{2,1,0:T(8,128)(2,1)S(1)}, u32[]{:S(2)}, u32[]{:S(2)}) %collective-permute-start.13) | collective-permute-done | bytes 393248 | tf_op jit(solution)/shard_map/ppermute | solution.py:154
  217.4 0.1 fusion.23
  217.5 0.1 collective-permute-start.15
  217.6 0.3 collective-permute-done.7
  217.9 0.1 fusion.26
  218.1 9.1 %collective-permute-done.15 = bf16[1,768,128]{2,1,0:T(8,128)(2,1)S(1)} collective-permute-done((bf16[1,768,128]{2,1,0:T(8,128)(2,1)S(1)}, bf16[1,768,128]{2,1,0:T(8,128)(2,1)S(1)}, u32[]{:S(2)}, u32[]{:S(2)}) %collective-permute-start.15) | collective-permute-done | bytes 196640 | tf_op jit(solution)/shard_map/ppermute | solution.py:154
  227.2 0.1 fusion.21
  227.4 0.9 copy.30
  (53 shorter events, 0.9 us)
Async XLA Ops:
  7.2 105.2 %all-gather.2.cloned.1.call-start = ((), (), s32[]{:S(2)}) async-start(), calls=%async_computation | async-start | bytes 6684672 | tf_op jit(solution)/shard_map/all_gather | solution.py:228
  9.8 7.3 %copy-start.3 = (bf16[128,1536]{1,0:T(8,128)(2,1)S(1)}, bf16[128,1536]{1,0:T(8,128)(2,1)}, u32[]{:S(2)}) copy-start(bf16[128,1536]{1,0:T(8,128)(2,1)} %param.8) | copy-start | bytes 1179652
  17.1 13.1 %copy-start.4 = (f32[3072]{0:T(1024)S(1)}, f32[3072]{0:T(1024)}, u32[]{:S(2)}) copy-start(f32[3072]{0:T(1024)} %param.9) | copy-start | bytes 36868
  49.1 9.4 %copy-start.5 = (s32[12]{0:T(128)S(1)}, s32[12]{0:T(128)}, u32[]{:S(2)}) copy-start(s32[12]{0:T(128)} %param.14) | copy-start | bytes 148
  49.1 9.4 %copy-start.2 = (s32[4]{0:T(128)S(1)}, s32[4]{0:T(128)}, u32[]{:S(2)}) copy-start(s32[4]{0:T(128)} %param.12) | copy-start | bytes 52
  49.1 10.2 %copy-start.6 = (s32[12]{0:T(128)S(1)}, s32[12]{0:T(128)}, u32[]{:S(2)}) copy-start(s32[12]{0:T(128)} %param.15) | copy-start | bytes 148
  112.4 2.3 copy-start
  114.7 2.3 copy-start.1
  142.9 3.6 %collective-permute-start.1 = (bf16[8,768,128]{2,1,0:T(8,128)(2,1)S(1)}, bf16[8,768,128]{2,1,0:T(8,128)(2,1)S(1)}, u32[]{:S(2)}, u32[]{:S(2)}) collective-permute-start(bf16[8,768,128]{2,1,0:T(8,128)(2,1)S(1)} %get-tuple-element.26), channel_id=1, source_target_pairs={{0,2},{2,0},{4,6},{6,4},{8,10},{10,8},{12,14},{14,12},{16,18},{18,... | collective-permute-start | bytes 4718600 | tf_op jit(solution)/shard_map/ppermute | solution.py:154
  143.0 3.5 %collective-permute-start = (f32[8,2,8,128]{3,2,1,0:T(8,128)S(1)}, f32[8,2,8,128]{3,2,1,0:T(8,128)S(1)}, u32[]{:S(2)}, u32[]{:S(2)}) collective-permute-start(f32[8,2,8,128]{3,2,1,0:T(8,128)S(1)} %get-tuple-element.25), channel_id=1, source_target_pairs={{0,2},{2,0},{4,6},{6,4},{8,10},{10,8},{12,14},{14,12},{16,18},{18,... | collective-permute-start | bytes 196616 | tf_op jit(solution)/shard_map/ppermute | solution.py:154
  147.1 4.0 %collective-permute-start.2 = (f32[4,2,8,128]{3,2,1,0:T(8,128)S(1)}, f32[4,2,8,128]{3,2,1,0:T(8,128)S(1)}, u32[]{:S(2)}, u32[]{:S(2)}) collective-permute-start(f32[4,2,8,128]{3,2,1,0:T(8,128)S(1)} %get-tuple-element.29), channel_id=1, source_target_pairs={{0,4},{2,6},{4,0},{6,2},{8,12},{10,14},{12,8},{14,10},{16,20},{18,... | collective-permute-start | bytes 98312 | tf_op jit(solution)/shard_map/ppermute | solution.py:154
  149.4 41.9 %collective-permute-start.3 = (bf16[4,768,128]{2,1,0:T(8,128)(2,1)S(1)}, bf16[4,768,128]{2,1,0:T(8,128)(2,1)S(1)}, u32[]{:S(2)}, u32[]{:S(2)}) collective-permute-start(bf16[4,768,128]{2,1,0:T(8,128)(2,1)S(1)} %get-tuple-element.30), channel_id=1, source_target_pairs={{0,4},{2,6},{4,0},{6,2},{8,12},{10,14},{12,8},{14,10},{16,20},{18,... | collective-permute-start | bytes 2359304 | tf_op jit(solution)/shard_map/ppermute | solution.py:154
  151.2 26.8 %collective-permute-start.4 = (f32[2,2,8,128]{3,2,1,0:T(8,128)S(1)}, f32[2,2,8,128]{3,2,1,0:T(8,128)S(1)}, u32[]{:S(2)}, u32[]{:S(2)}) collective-permute-start(f32[2,2,8,128]{3,2,1,0:T(8,128)S(1)} %pad_maximum_fusion.5), channel_id=1, source_target_pairs={{0,8},{2,10},{4,12},{6,14},{8,0},{10,2},{12,4},{14,6},{16,24},{18,... | collective-permute-start | bytes 49160 | tf_op jit(solution)/shard_map/ppermute | solution.py:154
  177.3 1.3 collective-permute-start.8
  177.4 9.7 %collective-permute-start.9 = (bf16[8,768,128]{2,1,0:T(8,128)(2,1)S(1)}, bf16[8,768,128]{2,1,0:T(8,128)(2,1)S(1)}, u32[]{:S(2)}, u32[]{:S(2)}) collective-permute-start(bf16[8,768,128]{2,1,0:T(8,128)(2,1)S(1)} %get-tuple-element.35), channel_id=1, source_target_pairs={{0,2},{2,0},{4,6},{6,4},{8,10},{10,8},{12,14},{14,12},{16,18},{18,... | collective-permute-start | bytes 4718600 | tf_op jit(solution)/shard_map/ppermute | solution.py:154
  178.7 4.0 %collective-permute-start.10 = (f32[4,2,8,128]{3,2,1,0:T(8,128)S(1)}, f32[4,2,8,128]{3,2,1,0:T(8,128)S(1)}, u32[]{:S(2)}, u32[]{:S(2)}) collective-permute-start(f32[4,2,8,128]{3,2,1,0:T(8,128)S(1)} %pad_maximum_fusion.4), channel_id=1, source_target_pairs={{0,4},{2,6},{4,0},{6,2},{8,12},{10,14},{12,8},{14,10},{16,20},{18,... | collective-permute-start | bytes 98312 | tf_op jit(solution)/shard_map/ppermute | solution.py:154
  178.8 4.6 %collective-permute-start.6 = (f32[1,2,8,128]{3,2,1,0:T(8,128)S(1)}, f32[1,2,8,128]{3,2,1,0:T(8,128)S(1)}, u32[]{:S(2)}, u32[]{:S(2)}) collective-permute-start(f32[1,2,8,128]{3,2,1,0:T(8,128)S(1)} %pad_maximum_fusion.7), channel_id=1, source_target_pairs={{0,16},{2,18},{4,20},{6,22},{8,24},{10,26},{12,28},{14,30},{16,0},... | collective-permute-start | bytes 24584 | tf_op jit(solution)/shard_map/ppermute | solution.py:154
  182.7 3.8 %collective-permute-start.12 = (f32[2,2,8,128]{3,2,1,0:T(8,128)S(1)}, f32[2,2,8,128]{3,2,1,0:T(8,128)S(1)}, u32[]{:S(2)}, u32[]{:S(2)}) collective-permute-start(f32[2,2,8,128]{3,2,1,0:T(8,128)S(1)} %pad_maximum_fusion.6), channel_id=1, source_target_pairs={{0,8},{2,10},{4,12},{6,14},{8,0},{10,2},{12,4},{14,6},{16,24},{18,... | collective-permute-start | bytes 49160 | tf_op jit(solution)/shard_map/ppermute | solution.py:154
  186.5 4.7 %collective-permute-start.14 = (f32[1,2,8,128]{3,2,1,0:T(8,128)S(1)}, f32[1,2,8,128]{3,2,1,0:T(8,128)S(1)}, u32[]{:S(2)}, u32[]{:S(2)}) collective-permute-start(f32[1,2,8,128]{3,2,1,0:T(8,128)S(1)} %pad_maximum_fusion.8), channel_id=1, source_target_pairs={{0,16},{2,18},{4,20},{6,22},{8,24},{10,26},{12,28},{14,30},{16,0},... | collective-permute-start | bytes 24584 | tf_op jit(solution)/shard_map/ppermute | solution.py:154
  187.4 17.4 %collective-permute-start.11 = (bf16[4,768,128]{2,1,0:T(8,128)(2,1)S(1)}, bf16[4,768,128]{2,1,0:T(8,128)(2,1)S(1)}, u32[]{:S(2)}, u32[]{:S(2)}) collective-permute-start(bf16[4,768,128]{2,1,0:T(8,128)(2,1)S(1)} %fusion.6), channel_id=1, source_target_pairs={{0,4},{2,6},{4,0},{6,2},{8,12},{10,14},{12,8},{14,10},{16,20},{18,... | collective-permute-start | bytes 2359304 | tf_op jit(solution)/shard_map/ppermute | solution.py:154
  191.5 15.5 %collective-permute-start.5 = (bf16[2,768,128]{2,1,0:T(8,128)(2,1)S(1)}, bf16[2,768,128]{2,1,0:T(8,128)(2,1)S(1)}, u32[]{:S(2)}, u32[]{:S(2)}) collective-permute-start(bf16[2,768,128]{2,1,0:T(8,128)(2,1)S(1)} %fusion.19), channel_id=1, source_target_pairs={{0,8},{2,10},{4,12},{6,14},{8,0},{10,2},{12,4},{14,6},{16,24},{18,... | collective-permute-start | bytes 1179656 | tf_op jit(solution)/shard_map/ppermute | solution.py:154
  205.2 12.2 %collective-permute-start.13 = (bf16[2,768,128]{2,1,0:T(8,128)(2,1)S(1)}, bf16[2,768,128]{2,1,0:T(8,128)(2,1)S(1)}, u32[]{:S(2)}, u32[]{:S(2)}) collective-permute-start(bf16[2,768,128]{2,1,0:T(8,128)(2,1)S(1)} %fusion.17), channel_id=1, source_target_pairs={{0,8},{2,10},{4,12},{6,14},{8,0},{10,2},{12,4},{14,6},{16,24},{18,... | collective-permute-start | bytes 1179656 | tf_op jit(solution)/shard_map/ppermute | solution.py:154
  207.1 10.8 %collective-permute-start.7 = (bf16[1,768,128]{2,1,0:T(8,128)(2,1)S(1)}, bf16[1,768,128]{2,1,0:T(8,128)(2,1)S(1)}, u32[]{:S(2)}, u32[]{:S(2)}) collective-permute-start(bf16[1,768,128]{2,1,0:T(8,128)(2,1)S(1)} %bitcast.166), channel_id=1, source_target_pairs={{0,16},{2,18},{4,20},{6,22},{8,24},{10,26},{12,28},{14,30},{16,0},... | collective-permute-start | bytes 589832 | tf_op jit(solution)/shard_map/ppermute | solution.py:154
  217.5 9.7 %collective-permute-start.15 = (bf16[1,768,128]{2,1,0:T(8,128)(2,1)S(1)}, bf16[1,768,128]{2,1,0:T(8,128)(2,1)S(1)}, u32[]{:S(2)}, u32[]{:S(2)}) collective-permute-start(bf16[1,768,128]{2,1,0:T(8,128)(2,1)S(1)} %bitcast.165), channel_id=1, source_target_pairs={{0,16},{2,18},{4,20},{6,22},{8,24},{10,26},{12,28},{14,30},{16,0},... | collective-permute-start | bytes 589832 | tf_op jit(solution)/shard_map/ppermute | solution.py:154
Sparse Core Ops, SparseCore 0:
  49.0 63.3 all-gather.1
